TPU v7x, 32 devices: a whole 2x2x4 slice. The times are simulated.
32 devices in a mesh: groups: 2 (over x), tensor: 8 (over z, y), role: 2 (over core).
Axes of the slice: x: 2, y: 2, z: 4, core: 2. Of those that a mesh axis runs over, the one named last changes fastest.
Arguments:
- context: bfloat16 [320, 8192], P('groups', ('tensor', 'role')), parts along dimension 0, may hold values from -6 to 6
- w_out: bfloat16 [8192, 8192], P(('tensor', 'role')), may hold values from -0.09375 to 0.09375
- residual: bfloat16 [320, 8192], P('groups', ('tensor', 'role')), parts along dimension 0, may hold values from -6 to 6
- fc_rest: bfloat16 [320, 8192], P('groups', ('tensor', 'role')), parts along dimension 0, may hold values from -6 to 6
- w_fc: bfloat16 [8192, 8192], P(None, ('tensor', 'role')), may hold values from -0.0625 to 0.0625
- norm_gain: float32 [8192], P(('tensor', 'role')), may hold values from 0.25 to 1.75
- w_lm: bfloat16 [8192, 16000], P(None, ('tensor', 'role')), may hold values from -0.0625 to 0.0625
- tokens: int32 [324], P('groups'), parts along dimension 0, may hold values from 0 to 128255
- segments: int32 [324], P('groups'), parts along dimension 0, may hold values from 0 to 3, never falling along the last dimension, each value on 1 to 80 neighbouring positions
- vocab_map: int32 [256512], P('groups'), parts along dimension 0, may hold values from -1 to 15999, as said below
Outputs:
- step_losses: float32 [4], P('groups'), parts along dimension 0
- grad_fc: bfloat16 [16384, 8192], P('groups', ('tensor', 'role')), parts along dimension 0
- grad_gain: float32 [16384], P(('groups', 'tensor', 'role')), parts along dimension 0
There are 2 independent parts, one for each index of `groups`. A program takes and returns all parts, laid end to end along the dimension named above; an argument that names none is the same for every part. Nothing has to cross between parts.
Inputs may be any that keep to these rules, and one draw needn't show every extreme that they name: `vocab_map`: each draft id 0 to 15999 appears exactly once; all other entries are -1.
All inputs are finite; a program needn't handle non-finite values.
Results may differ from a plain program's by a relative error of at most 0.0058.
Values may be sent and summed in bfloat16 or wider, within the bound.
A program may use at most 128 MiB of HBM per device.

v0:
```python
import jax
import jax.numpy as jnp
from jax import lax
from jax.sharding import PartitionSpec as P

EPS = 1e-05


def feature_total(values):
    return lax.psum(jnp.sum(values, axis=1), ("tensor", "role"))


def settle(state, norm_gain, full_width):
    inverse = lax.rsqrt(feature_total(state * state) / full_width + EPS)
    return ((state * inverse[:, None] * norm_gain).astype(jnp.bfloat16), inverse)


def unwind(state, inverse, grad_normed, norm_gain, full_width):
    scaled = norm_gain * grad_normed
    projection = feature_total(state * scaled) / full_width
    grad_state = inverse[:, None] * scaled - state * (inverse**3 * projection)[:, None]
    gain_grad = jnp.sum(grad_normed * state * inverse[:, None], axis=0)
    return (grad_state, gain_grad)


def on_device(
    context, w_out, residual, fc_rest, w_fc, norm_gain, w_lm, tokens, segments, vocab_map
):
    devices = lax.axis_size(("tensor", "role"))
    position = lax.axis_index(("tensor", "role"))
    tok_rows = tokens.shape[0] - 2
    own_cols = w_fc.shape[1]
    full_width = own_cols * devices
    vocab_own = w_lm.shape[1]
    partial_value = jnp.dot(context, w_out, preferred_element_type=jnp.float32)
    summed = lax.psum_scatter(partial_value, ("tensor", "role"), scatter_dimension=1, tiled=True)
    high_part = (summed + residual.astype(jnp.float32)).astype(jnp.bfloat16)
    captured = lax.all_gather(high_part, ("tensor", "role"), axis=1, tiled=True)
    features = fc_rest.astype(jnp.float32) + jnp.dot(
        captured, w_fc, preferred_element_type=jnp.float32
    )
    seg_now = segments[:tok_rows]
    follows = jnp.concatenate(
        [
            jnp.zeros((1,), jnp.float32),
            (segments[1:tok_rows] == segments[: tok_rows - 1]).astype(jnp.float32),
        ]
    )
    normed_one, scale_one = settle(features, norm_gain, full_width)
    shifted = jnp.concatenate(
        [jnp.zeros((1, own_cols), jnp.float32), normed_one[:-1].astype(jnp.float32)], axis=0
    )
    second = features + shifted * follows[:, None]
    normed_two, scale_two = settle(second, norm_gain, full_width)
    columns = position * vocab_own + jnp.arange(vocab_own, dtype=jnp.int32)

    def head(normed_part, shift, weight):
        normed = lax.all_gather(normed_part, ("tensor", "role"), axis=1, tiled=True)
        logits = jnp.dot(normed, w_lm, preferred_element_type=jnp.float32)
        powers = jnp.exp(logits)
        labels = vocab_map[tokens[shift : shift + tok_rows]]
        usable = ((labels >= 0) & (segments[shift : shift + tok_rows] == seg_now)).astype(
            jnp.float32
        )
        matches = columns[None, :] == labels[:, None]
        totals, picked = lax.psum(
            (jnp.sum(powers, axis=1), jnp.sum(jnp.where(matches, logits, 0.0), axis=1)),
            ("tensor", "role"),
        )
        average = jnp.sum(usable * (jnp.log(totals) - picked)) / jnp.maximum(jnp.sum(usable), 1.0)
        dlogits = (
            (weight * usable)[:, None] * (powers / totals[:, None] - matches.astype(jnp.float32))
        ).astype(jnp.bfloat16)
        head_part = jnp.einsum("tv,dv->td", dlogits, w_lm, preferred_element_type=jnp.float32)
        return (average, head_part)

    loss_one, part_one = head(normed_one, 1, 1.0)
    loss_two, part_two = head(normed_two, 2, 0.8)

    def vocab_sum(head_part):
        return lax.psum_scatter(head_part, ("tensor", "role"), scatter_dimension=1, tiled=True)

    head_two = vocab_sum(part_two)
    grad_two, gain_two = unwind(second, scale_two, head_two, norm_gain, full_width)
    head_one = vocab_sum(part_one)
    carried = head_one + jnp.concatenate(
        [grad_two[1:] * follows[1:, None], jnp.zeros((1, own_cols), jnp.float32)], axis=0
    )
    grad_one, gain_one = unwind(features, scale_one, carried, norm_gain, full_width)
    grad_fc = jnp.einsum(
        "ti,tj->ij",
        captured,
        (grad_one + grad_two).astype(jnp.bfloat16),
        preferred_element_type=jnp.float32,
    ).astype(jnp.bfloat16)
    return (jnp.stack([loss_one, loss_two]), grad_fc, gain_one + gain_two)


def solution(mesh):
    placed = (
        P("groups", ("tensor", "role")),
        P(("tensor", "role"), None),
        P("groups", ("tensor", "role")),
        P("groups", ("tensor", "role")),
        P(None, ("tensor", "role")),
        P(("tensor", "role")),
        P(None, ("tensor", "role")),
        P("groups"),
        P("groups"),
        P("groups"),
    )
    return jax.shard_map(
        on_device,
        mesh=mesh,
        in_specs=placed,
        out_specs=(P("groups"), P("groups", ("tensor", "role")), P(("groups", "tensor", "role"))),
        check_vma=False,
    )
```

profile of v0, /device:TPU:0, one launch (start us, length us, event | category | flops | bytes accessed | tf_op | source)
XLA Modules:
  0.0 589.8 jit_solution(7820374978905063894)
XLA Ops:
  7.3 7.5 %fusion.26 = f32[160,8192]{1,0:T(8,128)} fusion(bf16[160,512]{1,0:T(8,128)(2,1)} %param.10, bf16[512,8192]{1,0:T(8,128)(2,1)} %param.11), kind=kOutput, calls=%fused_computation.67 | convolution fusion | flops 1342177280 | bytes 13795328 | tf_op jit(solution)/shard_map/dot_general | solution.py:35
  14.8 81.2 %reduce-scatter.4.cloned.1.call-done = f32[160,512]{1,0:T(8,128)} async-done(((f32[160,8192]{1,0:T(8,128)}), f32[160,512]{1,0:T(8,128)}) %reduce-scatter.4.cloned.1.call-update) | async-done | bytes 327696 | tf_op jit(solution)/shard_map/reduce_scatter | solution.py:36
  96.0 1.7 add_convert_fusion.1
  97.9 43.8 %all-gather.4.cloned.1.call-done = bf16[160,8192]{1,0:T(8,128)(2,1)} async-done(((bf16[160,512]{1,0:T(8,128)(2,1)}), bf16[160,8192]{1,0:T(8,128)(2,1)}) %all-gather.4.cloned.1.call-update) | async-done | bytes 2621456 | tf_op jit(solution)/shard_map/all_gather | solution.py:38
  141.8 5.8 multiply_reduce_fusion.5
  147.6 31.3 %psum.56 = f32[160]{0:T(256)S(1)} all-reduce(f32[160]{0:T(256)S(1)} %get-tuple-element.30), channel_id=1, replica_groups=mesh['groups'=2,'tensor'=8,'role'=2] {'tensor','role'}, use_global_device_ids=true, to_apply=%region_2.0 | all-reduce | flops 160 | bytes 1280 | tf_op jit(solution)/shard_map/psum | solution.py:10
  179.2 29.5 %psum.59 = f32[160]{0:T(256)S(1)} all-reduce(f32[160]{0:T(256)S(1)} %get-tuple-element.24), channel_id=1, replica_groups=mesh['groups'=2,'tensor'=8,'role'=2] {'tensor','role'}, use_global_device_ids=true, to_apply=%region_10.11 | all-reduce | flops 160 | bytes 1280 | tf_op jit(solution)/shard_map/psum | solution.py:10
  208.7 0.8 multiply_convert_fusion
  209.5 0.5 all-gather.6.cloned.1.call-update
  210.2 1.4 gather_fusion.1
  211.7 1.4 gather_fusion
  213.2 37.7 %all-gather.8.cloned.1.call-done = bf16[160,8192]{1,0:T(8,128)(2,1)} async-done(((bf16[160,512]{1,0:T(8,128)(2,1)}), bf16[160,8192]{1,0:T(8,128)(2,1)}) %all-gather.8.cloned.1.call-update) | async-done | bytes 2621456 | tf_op jit(solution)/shard_map/all_gather | solution.py:58
  250.9 10.0 %fusion.27 = f32[160,1000]{1,0:T(8,128)S(1)} fusion(bf16[160,8192]{1,0:T(8,128)(2,1)} %all-gather.8.cloned.1.call-done, bf16[8192,1000]{0,1:T(8,128)(2,1)} %param.16), kind=kOutput, calls=%fused_computation.68 | convolution fusion | flops 2621440000 | bytes 19645440 | tf_op jit(solution)/shard_map/dot_general | solution.py:59
  261.0 34.6 %all-gather.6.cloned.1.call-done = bf16[160,8192]{1,0:T(8,128)(2,1)} async-done(((bf16[160,512]{1,0:T(8,128)(2,1)}), bf16[160,8192]{1,0:T(8,128)(2,1)}) %all-gather.6.cloned.1.call-update) | async-done | bytes 2621456 | tf_op jit(solution)/shard_map/all_gather | solution.py:58
  295.6 10.4 %exponential_reduce_fusion.1 = (f32[160]{0:T(256)S(1)}, f32[160]{0:T(256)S(1)}, f32[160]{0:T(256)S(1)}, f32[160]{0:T(256)S(1)}, f32[160,1000]{1,0:T(8,128)S(1)}) fusion(s32[160]{0:T(256)S(1)} %gather_fusion, s32[1000]{0:T(1024)S(1)} %iota_add_fusion, f32[160,1000]{1,0:T(8,128)S(1)} %fusion.27, s32[160]{0:T(256)S(1)} %gather_fusion.1, ...), kind=kOutput, calls=%fused_computation.17 | convolution fusion | flops 2622718976 | bytes 20293280 | tf_op jit(solution)/shard_map/dot_general | solution.py:59
  306.0 31.3 %psum.60 = f32[160]{0:T(256)S(1)} all-reduce(f32[160]{0:T(256)S(1)} %get-tuple-element.27), channel_id=1, replica_groups=mesh['groups'=2,'tensor'=8,'role'=2] {'tensor','role'}, use_global_device_ids=true, to_apply=%region_12.13 | all-reduce | flops 160 | bytes 1280 | tf_op jit(solution)/shard_map/psum | solution.py:66
  337.2 8.9 %fusion.8 = f32[160,8192]{1,0:T(8,128)} fusion(bf16[8192,1000]{0,1:T(8,128)(2,1)} %param.16, f32[160,1000]{1,0:T(8,128)S(1)} %fusion.27, f32[160]{0:T(256)S(1)} %psum.60, f32[160]{0:T(256)S(1)} %get-tuple-element.22, s32[1000]{0:T(1024)S(1)} %iota_add_fusion, s32[160]{0:T(256)S(1)} %gather_fusion.1), kind=kOutput, calls=%fused_computation.18 | convolution fusion | flops 2622400000 | bytes 22272800 | tf_op jit(solution)/shard_map/tv,dv->td/dot_general | solution.py:74
  346.3 75.7 %reduce-scatter.8.cloned.1.call-done = f32[160,512]{1,0:T(8,128)} async-done(((f32[160,8192]{1,0:T(8,128)}), f32[160,512]{1,0:T(8,128)}) %reduce-scatter.8.cloned.1.call-update) | async-done | bytes 327696 | tf_op jit(solution)/shard_map/reduce_scatter | solution.py:81
  422.0 1.1 multiply_reduce_fusion
  423.1 31.0 %all-reduce.3 = (f32[160]{0:T(256)S(1)}, f32[160]{0:T(256)S(1)}) all-reduce(f32[160]{0:T(256)S(1)} %get-tuple-element.7, f32[160]{0:T(256)S(1)} %get-tuple-element.6), channel_id=1, replica_groups=mesh['groups'=2,'tensor'=8,'role'=2] {'tensor','role'}, use_global_device_ids=true, to_apply=%region_4.0 | all-reduce | flops 320 | bytes 2560 | tf_op jit(solution)/shard_map/psum | solution.py:66
  454.1 8.9 %fusion.10 = f32[160,8192]{1,0:T(8,128)} fusion(bf16[8192,1000]{0,1:T(8,128)(2,1)} %param.16, f32[160,1000]{1,0:T(8,128)S(1)} %get-tuple-element.32, f32[160]{0:T(256)S(1)} %get-tuple-element.18, f32[160]{0:T(256)S(1)} %get-tuple-element.20, s32[1000]{0:T(1024)S(1)} %iota_add_fusion, s32[160]{0:T(256)S(1)} %gather_fusion), kind=kOutput, calls=%fused_computation.19 | convolution fusion | flops 2622400000 | bytes 22272800 | tf_op jit(solution)/shard_map/tv,dv->td/dot_general | solution.py:74
  463.1 1.2 multiply_subtract_fusion
  464.3 0.7 copy-done.5
  465.0 0.8 slice_multiply_fusion
  465.9 73.0 %reduce-scatter.6.cloned.1.call-done = f32[160,512]{1,0:T(8,128)} async-done(((f32[160,8192]{1,0:T(8,128)}), f32[160,512]{1,0:T(8,128)}) %reduce-scatter.6.cloned.1.call-update) | async-done | bytes 327696 | tf_op jit(solution)/shard_map/reduce_scatter | solution.py:81
  538.9 1.2 multiply_reduce_fusion.1
  540.1 30.8 %all-reduce.2 = (f32[160]{0:T(256)S(1)}, f32[160]{0:T(256)S(1)}, f32[160]{0:T(256)S(1)}) all-reduce(f32[160]{0:T(256)S(1)} %get-tuple-element.26, f32[160]{0:T(256)S(1)} %get-tuple-element.8, f32[160]{0:T(256)S(1)} %get-tuple-element.4), channel_id=1, replica_groups=mesh['groups'=2,'tensor'=8,'role'=2] {'tensor','role'}, use_global_device_ids=true, to_apply=%region_14.15 | all-reduce | flops 480 | bytes 3840 | tf_op jit(solution)/shard_map/psum | solution.py:66
  570.9 0.6 convert_reduce_fusion
  572.1 0.6 convert_reduce_fusion.1
  573.4 0.6 add.81
  575.3 0.6 pad_maximum_fusion.1
  575.9 7.1 %convolution_convert_fusion = bf16[8192,512]{1,0:T(8,128)(2,1)} fusion(bf16[160,8192]{1,0:T(8,128)(2,1)S(1)} %copy-done.2, f32[160,512]{1,0:T(8,128)} %copy-done.5, f32[160,512]{1,0:T(8,128)S(1)} %get-tuple-element.31, f32[160]{0:T(256)S(1)} %fusion.24, f32[512]{0:T(512)S(1)} %copy-done.9, f32[160]{0:T(256)S(1)} %add_rsqrt_fusion.1, ...), kind=kOutput, calls=%fused_computation.2 | convolution fusion | flops 1346945024 | bytes 12322048 | tf_op jit(solution)/shard_map/ti,tj->ij/dot_general | solution.py:90
  (47 shorter events, 1.1 us)
Async XLA Ops:
  7.2 203.0 %copy-start = (s32[128256]{0:T(1024)S(1)}, s32[128256]{0:T(1024)}, u32[]{:S(2)}) copy-start(s32[128256]{0:T(1024)} %param.19) | copy-start | bytes 1539076
  7.2 88.8 %copy-start.8 = (bf16[160,512]{1,0:T(8,128)(2,1)S(1)}, bf16[160,512]{1,0:T(8,128)(2,1)}, u32[]{:S(2)}) copy-start(bf16[160,512]{1,0:T(8,128)(2,1)} %param.12) | copy-start | bytes 491524
  7.2 90.6 %copy-start.10 = (s32[162]{0:T(256)S(1)}, s32[162]{0:T(256)}, u32[]{:S(2)}) copy-start(s32[162]{0:T(256)} %param.18) | copy-start | bytes 1948
  7.2 134.6 %copy-start.7 = (bf16[160,512]{1,0:T(8,128)(2,1)S(1)}, bf16[160,512]{1,0:T(8,128)(2,1)}, u32[]{:S(2)}) copy-start(bf16[160,512]{1,0:T(8,128)(2,1)} %param.13) | copy-start | bytes 491524
  7.2 88.8 %reduce-scatter.4.cloned.1.call-start = ((), (), s32[]{:S(2)}) async-start(), calls=%async_computation.3 | async-start | bytes 5570560 | tf_op jit(solution)/shard_map/reduce_scatter | solution.py:36
  14.7 127.0 %all-gather.4.cloned.1.call-start = ((), (), s32[]{:S(2)}) async-start(), calls=%async_computation.4 | async-start | bytes 2785280 | tf_op jit(solution)/shard_map/all_gather | solution.py:38
  97.7 153.2 %all-gather.8.cloned.1.call-start = ((), (), s32[]{:S(2)}) async-start(), calls=%async_computation.6 | async-start | bytes 2785280 | tf_op jit(solution)/shard_map/all_gather | solution.py:58
  97.9 80.9 %copy-start.9 = (f32[512]{0:T(512)S(1)}, f32[512]{0:T(512)}, u32[]{:S(2)}) copy-start(f32[512]{0:T(512)} %param.15) | copy-start | bytes 6148
  97.9 112.2 %copy-start.11 = (s32[162]{0:T(256)S(1)}, s32[162]{0:T(256)}, u32[]{:S(2)}) copy-start(s32[162]{0:T(256)} %param.17) | copy-start | bytes 1948
  178.9 30.6 %copy-start.6 = (bf16[160,512]{1,0:T(8,128)(2,1)}, bf16[160,512]{1,0:T(8,128)(2,1)S(1)}, u32[]{:S(2)}) copy-start(bf16[160,512]{1,0:T(8,128)(2,1)S(1)} %multiply_convert_fusion.1) | copy-start | bytes 491524
  179.2 242.8 %copy-start.3 = (f32[160,512]{1,0:T(8,128)}, f32[160,512]{1,0:T(8,128)S(1)}, u32[]{:S(2)}) copy-start(f32[160,512]{1,0:T(8,128)S(1)} %get-tuple-element.25) | copy-start | bytes 983044
  209.5 86.1 %all-gather.6.cloned.1.call-start = ((), (), s32[]{:S(2)}) async-start(), calls=%async_computation.5 | async-start | bytes 2785280 | tf_op jit(solution)/shard_map/all_gather | solution.py:58
  210.1 211.9 %reduce-scatter.8.cloned.1.call-start = ((), (), s32[]{:S(2)}) async-start(), calls=%async_computation.8 | async-start | bytes 5570560 | tf_op jit(solution)/shard_map/reduce_scatter | solution.py:81
  346.2 192.7 %reduce-scatter.6.cloned.1.call-start = ((), (), s32[]{:S(2)}) async-start(), calls=%async_computation.7 | async-start | bytes 5570560 | tf_op jit(solution)/shard_map/reduce_scatter | solution.py:81
  454.1 9.0 %copy-start.4 = (f32[160,512]{1,0:T(8,128)S(1)}, f32[160,512]{1,0:T(8,128)}, u32[]{:S(2)}) copy-start(f32[160,512]{1,0:T(8,128)} %copy-done.3) | copy-start | bytes 983044
  463.0 112.9 %copy-start.2 = (bf16[160,8192]{1,0:T(8,128)(2,1)S(1)}, bf16[160,8192]{1,0:T(8,128)(2,1)}, u32[]{:S(2)}) copy-start(bf16[160,8192]{1,0:T(8,128)(2,1)} %all-gather.4.cloned.1.call-done) | copy-start | bytes 7864324
  464.3 0.7 copy-start.5
  465.0 117.9 %copy-start.1 = (s32[128256]{0:T(1024)S(1)}, s32[128256]{0:T(1024)}, u32[]{:S(2)}) copy-start(s32[128256]{0:T(1024)} %param.19) | copy-start | bytes 1539076
Sparse Core Ops, SparseCore 0:
  14.9 81.0 reduce-scatter.3
  98.7 42.9 all-gather.3
  209.6 41.2 all-gather.7
  252.9 42.6 all-gather.5
  346.3 75.6 reduce-scatter.7
  463.2 75.6 reduce-scatter.5
where the time goes:
time: 590 us
  waiting for transfers between devices  347 us (59%)
  blocking collectives  154 us (26%)
  matrix products  58.6 us (10%)
  between operations  16.9 us (3%)
  other arithmetic  10 us (2%)
    reduce_scatter x2, waiting for transfers between devices, vocab_sum(): lax.psum_scatter(head_part, ('tensor', 'role'), scatter_dimension=1, tile...  149 us
    psum x3, blocking collectives, head(): lax.psum((jnp.sum(powers, axis=1), jnp.sum(jnp.where(matches, logits, 0.0...  93 us
    reduce_scatter x1, waiting for transfers between devices, on_device(): lax.psum_scatter(partial_value, ('tensor', 'role'), scatter_dimension=1,...  81.2 us
    all_gather x2, waiting for transfers between devices, head(): normed = lax.all_gather(normed_part, ('tensor', 'role'), axis=1, tiled=True)  72.4 us
    psum x2, blocking collectives, feature_total(): return lax.psum(jnp.sum(values, axis=1), ('tensor', 'role'))  60.8 us
    all_gather x1, waiting for transfers between devices, on_device(): captured = lax.all_gather(high_part, ('tensor', 'role'), axis=1, tiled=True)  43.8 us
    dot_general x2, matrix products, head(): logits = jnp.dot(normed, w_lm, preferred_element_type=jnp.float32)  20.4 us
    dot_general x2, matrix products, head(): jnp.einsum('tv,dv->td', dlogits, w_lm, preferred_element_type=jnp.float32)  17.9 us
  transfers between devices with their start and end apart: 6, of which 6 were waited for; matrix products, arithmetic and copies ran while one was open for 3% of the time, Pallas kernels for 0%

commit v1 on v0

v1 whole, which is shorter than its diff:
```python
import functools

import jax
import jax.numpy as jnp
from jax import lax
from jax.experimental import pallas as pl
from jax.experimental.pallas import tpu as pltpu
from jax.sharding import PartitionSpec as P

EPS = 1e-05
SHRINK = 1.0 / 1024.0
VMEM_BYTES = 56 * 1024 * 1024
EXTRA = 16
MESH = pl.DeviceIdType.MESH


def in_vmem():
    return pl.BlockSpec(memory_space=pltpu.VMEM)


def product(a, b):
    return jnp.dot(a, b, preferred_element_type=jnp.float32)


def greet(tensors, t, r):
    barrier = pltpu.get_barrier_semaphore()

    def hello(k, _):
        pl.semaphore_signal(
            barrier, inc=1, device_id={"tensor": lax.rem(t + k, tensors)}, device_id_type=MESH
        )
        return 0

    lax.fori_loop(1, tensors, hello, 0)
    pl.semaphore_signal(barrier, inc=1, device_id={"role": 1 - r}, device_id_type=MESH)
    pl.semaphore_wait(barrier, tensors)


def to_peer(src, dst, send_sem, recv_sem, peer):
    return pltpu.make_async_remote_copy(
        src_ref=src, dst_ref=dst, send_sem=send_sem, recv_sem=recv_sem,
        device_id={"tensor": peer}, device_id_type=MESH,
    )


def to_sibling(src, dst, send_sem, recv_sem, r):
    return pltpu.make_async_remote_copy(
        src_ref=src, dst_ref=dst, send_sem=send_sem, recv_sem=recv_sem,
        device_id={"role": 1 - r}, device_id_type=MESH,
    )


def scatter_sum(tensors, t, r, part, narrow, bufs, sems, total):
    pair_out, pair_in, out, inn = bufs
    pair_send, pair_recv, send, recv = sems

    def pair(d):
        return to_sibling(pair_out.at[d], pair_in.at[d], pair_send.at[d], pair_recv.at[d], r)

    def ahead(d):
        pair_out[d] = part(2 * d + 1 - r)
        pair(d).start()

    ahead(lax.rem(t + 1, tensors))

    def step(k, _):
        d = lax.rem(t + 1 + k, tensors)
        ahead(lax.rem(t + 2 + k, tensors))
        own = part(2 * d + r)
        pair(d).wait_recv()
        out[d] = narrow(own + pair_in[d])
        to_peer(out.at[d], inn.at[t], send.at[d], recv.at[t], d).start()
        return 0

    lax.fori_loop(0, tensors - 1, step, 0)
    own = part(2 * t + r)
    pair(t).wait_recv()
    total[...] = own + pair_in[t]

    def collect(k, _):
        s = lax.rem(t + tensors - k, tensors)
        to_peer(out.at[s], inn.at[s], send.at[s], recv.at[s], s).wait_recv()
        total[...] += inn[s].astype(jnp.float32)
        return 0

    lax.fori_loop(1, tensors, collect, 0)

    def finish(k, _):
        s = lax.rem(t + k, tensors)
        to_peer(out.at[s], inn.at[t], send.at[s], recv.at[t], s).wait_send()
        pair(s).wait_send()
        return 0

    lax.fori_loop(1, tensors, finish, 0)
    pair(t).wait_send()


def gather_blocks(tensors, t, r, buf, sems, use):
    send, recv, pair_send, pair_recv = sems
    mine = 2 * t + r

    def spread(k, _):
        d = lax.rem(t + k, tensors)
        to_peer(buf.at[mine], buf.at[mine], send.at[d], recv.at[t], d).start()
        return 0

    lax.fori_loop(1, tensors, spread, 0)

    def pair(s, q):
        return to_sibling(buf.at[q], buf.at[q], pair_send.at[s], pair_recv.at[s], r)

    pair(t, mine).start()
    use(mine)

    def near(k, _):
        s = lax.rem(t + tensors - k, tensors)
        q = 2 * s + r
        to_peer(buf.at[q], buf.at[q], send.at[s], recv.at[s], s).wait_recv()
        pair(s, q).start()
        use(q)
        return 0

    lax.fori_loop(1, tensors, near, 0)

    def far(k, _):
        s = lax.rem(t + tensors - k, tensors)
        q = 2 * s + 1 - r
        pair(s, q).wait_recv()
        use(q)
        return 0

    lax.fori_loop(0, tensors, far, 0)

    def finish(k, _):
        s = lax.rem(t + k, tensors)
        to_peer(buf.at[mine], buf.at[mine], send.at[s], recv.at[t], s).wait_send()
        pair(s, 2 * s + r).wait_send()
        return 0

    lax.fori_loop(1, tensors, finish, 0)
    pair(t, mine).wait_send()


def front_kernel(
    tensors, context, w_out, residual, fc_rest, w_fc, captured, features,
    pair_out, pair_in, out, inn, total, cap_buf, feat_buf, *sems,
):
    t, r = lax.axis_index("tensor"), lax.axis_index("role")
    cols = w_fc.shape[1]
    mine = 2 * t + r
    greet(tensors, t, r)

    def part(q):
        return product(context[...], w_out[:, pl.ds(pl.multiple_of(q * cols, cols), cols)])

    scatter_sum(
        tensors, t, r, part, lambda x: x.astype(jnp.bfloat16),
        (pair_out, pair_in, out, inn), sems[:4], total,
    )
    cap_buf[mine] = (total[...] + residual[...].astype(jnp.float32)).astype(jnp.bfloat16)
    total[...] = fc_rest[...].astype(jnp.float32)

    def multiply(q):
        block = cap_buf[q]
        captured[q] = block
        total[...] += product(block, w_fc[pl.ds(pl.multiple_of(q * cols, cols), cols), :])

    gather_blocks(tensors, t, r, cap_buf, sems[4:8], multiply)
    feat_buf[mine] = total[...].astype(jnp.bfloat16)

    def place(q):
        features[:, pl.ds(pl.multiple_of(q * cols, cols), cols)] = feat_buf[q]

    gather_blocks(tensors, t, r, feat_buf, sems[8:12], place)


def front(tensors, context, w_out, residual, fc_rest, w_fc):
    rows = context.shape[0]
    width, cols = w_fc.shape
    blocks = 2 * tensors
    return pl.pallas_call(
        functools.partial(front_kernel, tensors),
        out_shape=(
            jax.ShapeDtypeStruct((blocks, rows, cols), jnp.bfloat16),
            jax.ShapeDtypeStruct((rows, width), jnp.bfloat16),
        ),
        in_specs=[in_vmem()] * 5,
        out_specs=(in_vmem(), in_vmem()),
        scratch_shapes=[
            pltpu.VMEM((tensors, rows, cols), jnp.float32),
            pltpu.VMEM((tensors, rows, cols), jnp.float32),
            pltpu.VMEM((tensors, rows, cols), jnp.bfloat16),
            pltpu.VMEM((tensors, rows, cols), jnp.bfloat16),
            pltpu.VMEM((rows, cols), jnp.float32),
            pltpu.VMEM((blocks, rows, cols), jnp.bfloat16),
            pltpu.VMEM((blocks, rows, cols), jnp.bfloat16),
        ]
        + [pltpu.SemaphoreType.DMA((tensors,))] * 12,
        compiler_params=pltpu.CompilerParams(
            collective_id=0, has_side_effects=True, vmem_limit_bytes=VMEM_BYTES
        ),
    )(context, w_out, residual, fc_rest, w_fc)


def stats_kernel(tensors, stats, summed, buf, send, recv):
    t, r = lax.axis_index("tensor"), lax.axis_index("role")
    blocks = 2 * tensors
    mine = 2 * t + r
    barrier = pltpu.get_barrier_semaphore()

    def where(k):
        q = lax.rem(mine + k, blocks)
        return q, {"tensor": q // 2, "role": lax.rem(q, 2)}

    def hello(k, _):
        pl.semaphore_signal(barrier, inc=1, device_id=where(k)[1], device_id_type=MESH)
        return 0

    lax.fori_loop(1, blocks, hello, 0)
    pl.semaphore_wait(barrier, blocks - 1)

    def copy(q, slot, target):
        return pltpu.make_async_remote_copy(
            src_ref=stats, dst_ref=buf.at[slot], send_sem=send.at[q], recv_sem=recv.at[slot],
            device_id=target, device_id_type=MESH,
        )

    def spread(k, _):
        q, target = where(k)
        copy(q, mine, target).start()
        return 0

    lax.fori_loop(1, blocks, spread, 0)
    buf[mine] = stats[...]

    def collect(k, _):
        q, target = where(k)
        copy(q, q, target).wait_recv()
        copy(q, mine, target).wait_send()
        return 0

    lax.fori_loop(1, blocks, collect, 0)
    summed[...] = jnp.sum(buf[...], axis=0)


def group_sum(tensors, stats):
    blocks = 2 * tensors
    return pl.pallas_call(
        functools.partial(stats_kernel, tensors),
        out_shape=jax.ShapeDtypeStruct(stats.shape, jnp.float32),
        in_specs=[in_vmem()],
        out_specs=in_vmem(),
        scratch_shapes=[
            pltpu.VMEM((blocks,) + stats.shape, jnp.float32),
            pltpu.SemaphoreType.DMA((blocks,)),
            pltpu.SemaphoreType.DMA((blocks,)),
        ],
        compiler_params=pltpu.CompilerParams(
            collective_id=1, has_side_effects=True, vmem_limit_bytes=VMEM_BYTES
        ),
    )(stats)


def back_kernel(
    tensors, dlogits, w_lm, scales, gain, features, summed, pair_out, pair_in, out, inn, *sems
):
    t, r = lax.axis_index("tensor"), lax.axis_index("role")
    rows, cols = features.shape[0], out.shape[2]
    greet(tensors, t, r)
    line = lax.broadcasted_iota(jnp.int32, (EXTRA, cols), 0)

    def part(q):
        span = pl.ds(pl.multiple_of(q * cols, cols), cols)
        grads = lax.dot_general(
            dlogits[...], w_lm[span, :], (((1,), (1,)), ((), ())), preferred_element_type=jnp.float32
        )
        one, two = grads[:rows], grads[rows:]
        level = gain[:, span]
        here = scales[:, 0:1] * one + scales[:, 1:2] * two
        later = scales[:, 2:3] * pltpu.roll(two, rows - 1, 0) * level
        gain_part = jnp.sum(
            features[:, span].astype(jnp.float32) * (here + 2.0 * later), axis=0, keepdims=True
        )
        return jnp.concatenate(
            [level * (here + later), jnp.where(line == 0, gain_part, 0.0)], axis=0
        )

    def narrow(x):
        gain_row = x[rows : rows + 1]
        high = gain_row.astype(jnp.bfloat16).astype(jnp.float32)
        tail = jnp.where(line == 0, high, jnp.where(line == 1, gain_row - high, 0.0))
        return jnp.concatenate([x[:rows], tail], axis=0).astype(jnp.bfloat16)

    scatter_sum(tensors, t, r, part, narrow, (pair_out, pair_in, out, inn), sems, summed)


def back(tensors, dlogits, w_lm, scales, gain, features):
    rows, width = features.shape
    cols = width // (2 * tensors)
    tall = rows + EXTRA
    return pl.pallas_call(
        functools.partial(back_kernel, tensors),
        out_shape=jax.ShapeDtypeStruct((tall, cols), jnp.float32),
        in_specs=[in_vmem()] * 5,
        out_specs=in_vmem(),
        scratch_shapes=[
            pltpu.VMEM((tensors, tall, cols), jnp.float32),
            pltpu.VMEM((tensors, tall, cols), jnp.float32),
            pltpu.VMEM((tensors, tall, cols), jnp.bfloat16),
            pltpu.VMEM((tensors, tall, cols), jnp.bfloat16),
        ]
        + [pltpu.SemaphoreType.DMA((tensors,))] * 4,
        compiler_params=pltpu.CompilerParams(
            collective_id=2, has_side_effects=True, vmem_limit_bytes=VMEM_BYTES
        ),
    )(dlogits, w_lm, scales, gain, features)


def later_row(x):
    return jnp.concatenate([x[1:], jnp.zeros_like(x[:1])], axis=0)


def earlier_row(x):
    return jnp.concatenate([jnp.zeros_like(x[:1]), x[:-1]], axis=0)


def on_device(
    context, w_out, residual, fc_rest, w_fc, norm_gain, w_lm, tokens, segments, vocab_map
):
    tensors = lax.axis_size("tensor")
    position = lax.axis_index(("tensor", "role"))
    rows = tokens.shape[0] - 2
    width, cols = w_fc.shape
    vocab_own = w_lm.shape[1]

    gain = lax.all_gather(norm_gain, ("tensor", "role"), axis=0, tiled=True)[None, :]
    seg_now = segments[:rows]
    follows = jnp.concatenate(
        [
            jnp.zeros((1,), jnp.float32),
            (segments[1:rows] == segments[: rows - 1]).astype(jnp.float32),
        ]
    )
    labels_all = vocab_map[tokens]
    columns = position * vocab_own + jnp.arange(vocab_own, dtype=jnp.int32)

    captured, features = front(tensors, context, w_out, residual, fc_rest, w_fc)

    state = features.astype(jnp.float32)
    scale_one = lax.rsqrt(jnp.sum(state * state, axis=1) / width + EPS)
    normed_one = (state * scale_one[:, None] * gain).astype(jnp.bfloat16)
    shifted = earlier_row(normed_one).astype(jnp.float32) * follows[:, None]
    second = state + shifted
    scale_two = lax.rsqrt(jnp.sum(second * second, axis=1) / width + EPS)
    normed_two = (second * scale_two[:, None] * gain).astype(jnp.bfloat16)
    cross = jnp.sum(shifted * second, axis=1) / width

    logits = product(jnp.concatenate([normed_one, normed_two], axis=0), w_lm)
    logits_one, logits_two = logits[:rows], logits[rows:]

    def label_set(shift):
        labels = labels_all[shift : shift + rows]
        usable = ((labels >= 0) & (segments[shift : shift + rows] == seg_now)).astype(jnp.float32)
        return columns[None, :] == labels[:, None], usable

    matches_one, usable_one = label_set(1)
    matches_two, usable_two = label_set(2)
    powers_one, powers_two = jnp.exp(logits_one), jnp.exp(logits_two)

    def over(values):
        return jnp.sum(values, axis=1)

    stats = jnp.stack(
        [
            over(powers_one),
            over(powers_two),
            over(powers_one * (logits_one * SHRINK)),
            over(powers_two * (logits_two * SHRINK)),
            over(powers_two * (logits_one * SHRINK)),
            over(jnp.where(matches_one, logits_one, 0.0)),
            over(jnp.where(matches_two, logits_two, 0.0)),
            over(jnp.where(matches_two, logits_one, 0.0)),
        ]
    )
    (totals_one, totals_two, mean_one, mean_two, mean_mixed, picked_one, picked_two, picked_mixed) = (
        group_sum(tensors, stats)
    )

    def average(totals, picked, usable):
        return jnp.sum(usable * (jnp.log(totals) - picked)) / jnp.maximum(jnp.sum(usable), 1.0)

    losses = jnp.stack(
        [average(totals_one, picked_one, usable_one), average(totals_two, picked_two, usable_two)]
    )

    def gradient(powers, totals, matches, weight):
        return (
            weight[:, None] * (powers / totals[:, None] - matches.astype(jnp.float32))
        ).astype(jnp.bfloat16)

    weight_one, weight_two = usable_one, 0.8 * usable_two
    dlogits = jnp.concatenate(
        [
            gradient(powers_one, totals_one, matches_one, weight_one),
            gradient(powers_two, totals_two, matches_two, weight_two),
        ],
        axis=0,
    )
    follows_next = later_row(follows)
    link = scale_one * follows_next * later_row(scale_two)
    scales = jnp.stack([scale_one, scale_two, link], axis=1)
    summed = back(tensors, dlogits, w_lm, scales, gain, features)

    dot_one = weight_one * (mean_one / (SHRINK * totals_one) - picked_one)
    dot_two = weight_two * (mean_two / (SHRINK * totals_two) - picked_two)
    dot_mixed = weight_two * (mean_mixed / (SHRINK * totals_two) - picked_mixed)
    projection_two = dot_two / (scale_two * width)
    pull_two = scale_two**3 * projection_two
    back_link = follows * (dot_two / scale_two - dot_mixed / scale_one) / width
    through = later_row(follows * (scale_two * back_link - pull_two * cross))
    projection_one = (dot_one / width + through) / scale_one
    pull_one = scale_one**3 * projection_one

    own = position * cols
    state_own = lax.dynamic_slice_in_dim(features, own, cols, axis=1).astype(jnp.float32)
    normed_own = lax.dynamic_slice_in_dim(normed_one, own, cols, axis=1).astype(jnp.float32)
    second_own = state_own + earlier_row(normed_own) * follows[:, None]
    pulled = later_row(second_own * (follows * pull_two)[:, None]) * scale_one[:, None]
    gradient_sum = (
        summed[:rows]
        - norm_gain[None, :] * pulled
        - state_own * pull_one[:, None]
        - second_own * pull_two[:, None]
    ).astype(jnp.bfloat16)
    grad_gain = summed[rows] + summed[rows + 1] - jnp.sum(pulled * state_own, axis=0)
    grad_fc = (
        jnp.einsum("pti,tj->pij", captured, gradient_sum, preferred_element_type=jnp.float32)
        .astype(jnp.bfloat16)
        .reshape(width, cols)
    )
    return (losses, grad_fc, grad_gain)


def solution(mesh):
    placed = (
        P("groups", ("tensor", "role")),
        P(("tensor", "role"), None),
        P("groups", ("tensor", "role")),
        P("groups", ("tensor", "role")),
        P(None, ("tensor", "role")),
        P(("tensor", "role")),
        P(None, ("tensor", "role")),
        P("groups"),
        P("groups"),
        P("groups"),
    )
    return jax.shard_map(
        on_device,
        mesh=mesh,
        in_specs=placed,
        out_specs=(P("groups"), P("groups", ("tensor", "role")), P(("groups", "tensor", "role"))),
        check_vma=False,
    )
```

time: 590 us -> 253 us (0.43)
  the two profiles are of different devices: /device:TPU:0 before, /device:TPU:15 now
where the time goes in v1:
time: 253 us; the launch traced here: 252 us
  Pallas kernels  167 us (66%)
  local copies, waits for them, and re-layouts  27.4 us (11%)
  other arithmetic  19.7 us (8%)
  matrix products  17.8 us (7%)
  blocking collectives  16.8 us (7%)
  between operations  3.42 us (1%)
    pallas_call x1, Pallas kernels, front(): pl.pallas_call(functools.partial(front_kernel, tensors), out_shape=(jax.S...  106 us
    pallas_call x1, Pallas kernels, back(): pl.pallas_call(functools.partial(back_kernel, tensors), out_shape=jax.Sha...  47.4 us
    unnamed x17, local copies, waits for them, and re-layouts  22.4 us
    all_gather x1, blocking collectives, on_device(): lax.all_gather(norm_gain, ('tensor', 'role'), axis=0, tiled=True)[None, :]  16.8 us
    pallas_call x1, Pallas kernels, group_sum(): pl.pallas_call(functools.partial(stats_kernel, tensors), out_shape=jax.Sh...  13.7 us
    dot_general x1, matrix products, product(): return jnp.dot(a, b, preferred_element_type=jnp.float32)  10.8 us
    dot_general x1, matrix products, on_device(): jnp.einsum('pti,tj->pij', captured, gradient_sum, preferred_element_type=...  6.98 us

profile of v1, /device:TPU:15, one launch (start us, length us, event | category | flops | bytes accessed | tf_op | source)
XLA Modules:
  0.0 252.3 jit_solution(7509223628877647297)
XLA Ops:
  0.7 106.1 %shard_map.121 = (bf16[16,160,512]{2,1,0:T(8,128)(2,1)}, bf16[160,8192]{1,0:T(8,128)(2,1)}) custom-call(bf16[160,512]{1,0:T(8,128)(2,1)} %context.1, bf16[512,8192]{1,0:T(8,128)(2,1)} %w_out.1, bf16[160,512]{1,0:T(8,128)(2,1)} %residual.1, bf16[160,512]{1,0:T(8,128)(2,1)} %fc_rest.1, bf16[8192,512]{1,0:T(8,128)(2,1)} %w_fc.1), custom_call_target="tpu_custom_call" | custom-call | tf_op jit(solution)/shard_map/pallas_call | solution.py:181
  106.8 0.1 compare_convert_fusion.2
  106.9 0.1 pad_maximum_fusion.4
  106.9 16.8 %all-gather = f32[16,1,512]{2,1,0:T(1,128)S(1)} all-gather(f32[1,1,512]{2,1,0:T(1,128)S(1)} %bitcast.53), channel_id=1, replica_groups=mesh['groups'=2,'tensor'=8,'role'=2] {'tensor','role'}, dimensions={0}, use_global_device_ids=true | all-gather | bytes 34816 | tf_op jit(solution)/shard_map/all_gather | solution.py:336
  123.8 2.4 fusion
  126.1 2.5 fusion.2
  128.6 2.2 multiply_reduce_fusion
  130.9 3.1 %multiply_convert_fusion = bf16[160,8192]{1,0:T(8,128)(2,1)} fusion(bf16[160,8192]{1,0:T(8,128)(2,1)S(1)} %copy-done.1, f32[160]{0:T(256)S(1)} %add_rsqrt_fusion, f32[160]{0:T(256)S(1)} %pad_maximum_fusion.4, f32[8192]{0:T(1024)S(1)} %bitcast.37, bf16[159,8192]{1,0:T(8,128)(2,1)S(1)} %bitcast.34), kind=kLoop, calls=%fused_computation.13 | loop fusion | flops 9175040 | bytes 7881984 | tf_op jit(solution)/shard_map/convert_element_type | solution.py:355
  134.0 10.8 %fusion.3 = f32[320,1000]{1,0:T(8,128)} fusion(bf16[8192,1000]{0,1:T(8,128)(2,1)} %param.16, bf16[160,8192]{1,0:T(8,128)(2,1)} %multiply_convert_fusion, bf16[160,8192]{1,0:T(8,128)(2,1)S(1)} %fusion.2), kind=kOutput, calls=%fused_computation.8 | convolution fusion | flops 5253365760 | bytes 22906880 | tf_op jit(solution)/shard_map/dot_general | solution.py:22
  144.9 1.4 gather_fusion
  146.4 2.1 fusion.12
  148.5 0.6 stack.50.stats
  149.1 13.7 %shard_map.122 = f32[8,160]{1,0:T(8,128)} custom-call(f32[8,160]{1,0:T(8,128)} %stack.50.stats), custom_call_target="tpu_custom_call" | custom-call | tf_op jit(solution)/shard_map/pallas_call | solution.py:248
  162.8 1.0 fusion.37
  163.8 0.1 subtract_multiply_fusion.1
  163.9 0.6 subtract_multiply_fusion
  165.8 0.1 fusion.30
  165.9 0.6 convert_reduce_fusion.1
  167.8 0.6 pad_maximum_fusion.5
  168.4 0.9 constant_dynamic-slice_fusion
  169.4 0.1 convert_add_fusion.1
  169.5 1.7 fusion.10
  171.2 0.9 pad_maximum_fusion.dlogits
  172.1 22.4 %copy.20.w_lm = bf16[8192,1000]{1,0:T(8,128)(2,1)} copy(bf16[8192,1000]{0,1:T(8,128)(2,1)} %param.16) | data formatting | bytes 32768000 | tf_op args[6]
  194.5 0.1 fusion.28
  194.6 0.8 copy.21.scales
  195.3 47.4 %shard_map.123 = f32[176,512]{1,0:T(8,128)} custom-call(bf16[320,1000]{1,0:T(8,128)(2,1)} %pad_maximum_fusion.dlogits, bf16[8192,1000]{1,0:T(8,128)(2,1)} %copy.20.w_lm, f32[160,3]{1,0:T(8,128)} %copy.21.scales, f32[1,8192]{1,0:T(1,128)} %bitcast.38, bf16[160,8192]{1,0:T(8,128)(2,1)} %get-tuple-element.5.features), custom_call_target="tpu_custom_call" | custom-call | tf_op jit(solution)/shard_map/pallas_call | solution.py:301
  242.8 0.1 slice_multiply_fusion
  242.9 7.0 %convolution_convert_fusion = bf16[16,512,512]{2,1,0:T(8,128)(2,1)} fusion(bf16[16,160,512]{2,1,0:T(8,128)(2,1)S(1)} %copy-done.3, f32[160,512]{1,0:T(8,128)S(1)} %convert_add_fusion.1, f32[176,512]{1,0:T(8,128)} %shard_map.123, f32[159,512]{1,0:T(8,128)S(1)} %slice_multiply_fusion, f32[160]{0:T(256)S(1)} %get-tuple-element.24, ...), kind=kOutput, calls=%fused_computation.4 | convolution fusion | flops 1347108864 | bytes 12158852 | tf_op jit(solution)/shard_map/pti,tj->pij/dot_general | solution.py:437
  249.9 0.8 slice_add_fusion
  250.7 1.0 fusion.20
  251.8 0.6 sub.51
  (27 shorter events, 0.4 us)
Async XLA Ops:
  0.6 144.3 %copy-start = (s32[128256]{0:T(1024)S(1)}, s32[128256]{0:T(1024)}, u32[]{:S(2)}) copy-start(s32[128256]{0:T(1024)} %param.19) | copy-start | bytes 1539076
  0.6 106.1 %copy-start.5 = (s32[162]{0:T(256)S(1)}, s32[162]{0:T(256)}, u32[]{:S(2)}) copy-start(s32[162]{0:T(256)} %param.18) | copy-start | bytes 1948
  0.7 106.3 %copy-start.6 = (f32[512]{0:T(512)S(1)}, f32[512]{0:T(512)}, u32[]{:S(2)}) copy-start(f32[512]{0:T(512)} %param.15) | copy-start | bytes 6148
  106.8 21.8 %copy-start.1 = (bf16[160,8192]{1,0:T(8,128)(2,1)S(1)}, bf16[160,8192]{1,0:T(8,128)(2,1)}, u32[]{:S(2)}) copy-start(bf16[160,8192]{1,0:T(8,128)(2,1)} %get-tuple-element.5.features) | copy-start | bytes 7864324
  123.8 7.1 %copy-start.4 = (f32[16,1,512]{2,1,0:T(1,128)}, f32[16,1,512]{2,1,0:T(1,128)S(1)}, u32[]{:S(2)}) copy-start(f32[16,1,512]{2,1,0:T(1,128)S(1)} %all-gather) | copy-start | bytes 98308
  128.6 5.4 %copy-start.2 = (bf16[160,8192]{1,0:T(8,128)(2,1)}, bf16[160,8192]{1,0:T(8,128)(2,1)S(1)}, u32[]{:S(2)}) copy-start(bf16[160,8192]{1,0:T(8,128)(2,1)S(1)} %fusion.2) | copy-start | bytes 7864324
  134.0 10.9 %copy-start.7 = (s32[162]{0:T(256)S(1)}, s32[162]{0:T(256)}, u32[]{:S(2)}) copy-start(s32[162]{0:T(256)} %param.17) | copy-start | bytes 1948
  195.3 47.6 %copy-start.3 = (bf16[16,160,512]{2,1,0:T(8,128)(2,1)S(1)}, bf16[16,160,512]{2,1,0:T(8,128)(2,1)}, u32[]{:S(2)}) copy-start(bf16[16,160,512]{2,1,0:T(8,128)(2,1)} %get-tuple-element.6) | copy-start | bytes 7864324

commit v2 on v1

--- a/solution.py
+++ b/solution.py
@@ -22,159 +22,317 @@
     return jnp.dot(a, b, preferred_element_type=jnp.float32)
 
 
-def greet(tensors, t, r):
-    barrier = pltpu.get_barrier_semaphore()
-
-    def hello(k, _):
-        pl.semaphore_signal(
-            barrier, inc=1, device_id={"tensor": lax.rem(t + k, tensors)}, device_id_type=MESH
-        )
-        return 0
-
-    lax.fori_loop(1, tensors, hello, 0)
-    pl.semaphore_signal(barrier, inc=1, device_id={"role": 1 - r}, device_id_type=MESH)
-    pl.semaphore_wait(barrier, tensors)
-
-
-def to_peer(src, dst, send_sem, recv_sem, peer):
+class Place:
+    def __init__(self, tensors):
+        self.lanes = 2 if tensors == 8 else 1
+        self.depth = tensors // self.lanes
+        self.tensors = tensors
+        self.t, self.r = lax.axis_index("tensor"), lax.axis_index("role")
+        self.z, self.y = self.t // self.lanes, lax.rem(self.t, self.lanes)
+        self.mine = 2 * self.t + self.r
+
+    def before(self, k):
+        return lax.rem(self.z + self.depth - k, self.depth)
+
+    def after(self, k):
+        return lax.rem(self.z + k, self.depth)
+
+    def across(self, z):
+        return z * 2 + 1 - self.y
+
+    def along(self, z):
+        return z * self.lanes + self.y
+
+    def neighbours(self):
+        others = [{"role": 1 - self.r}]
+        if self.lanes == 2:
+            others.append({"tensor": self.across(self.z)})
+        return others
+
+    def greet(self):
+        barrier = pltpu.get_barrier_semaphore()
+
+        def hello(k, _):
+            pl.semaphore_signal(
+                barrier, inc=1, device_id={"tensor": self.along(self.after(k))}, device_id_type=MESH
+            )
+            return 0
+
+        lax.fori_loop(1, self.depth, hello, 0)
+        for other in self.neighbours():
+            pl.semaphore_signal(barrier, inc=1, device_id=other, device_id_type=MESH)
+        pl.semaphore_wait(barrier, self.depth - 1 + len(self.neighbours()))
+
+
+def remote(src, dst, send_sem, recv_sem, target):
     return pltpu.make_async_remote_copy(
         src_ref=src, dst_ref=dst, send_sem=send_sem, recv_sem=recv_sem,
-        device_id={"tensor": peer}, device_id_type=MESH,
-    )
-
-
-def to_sibling(src, dst, send_sem, recv_sem, r):
-    return pltpu.make_async_remote_copy(
-        src_ref=src, dst_ref=dst, send_sem=send_sem, recv_sem=recv_sem,
-        device_id={"role": 1 - r}, device_id_type=MESH,
-    )
-
-
-def scatter_sum(tensors, t, r, part, narrow, bufs, sems, total):
-    pair_out, pair_in, out, inn = bufs
-    pair_send, pair_recv, send, recv = sems
+        device_id=target, device_id_type=MESH,
+    )
+
+
+def scatter_scratch(tensors, rows, cols):
+    depth = tensors // (2 if tensors == 8 else 1)
+    return [
+        pltpu.VMEM((tensors, rows, cols), jnp.float32),
+        pltpu.VMEM((tensors, rows, cols), jnp.float32),
+        pltpu.VMEM((depth, rows, cols), jnp.bfloat16),
+        pltpu.VMEM((depth, rows, cols), jnp.bfloat16),
+        pltpu.VMEM((depth, rows, cols), jnp.bfloat16),
+        pltpu.VMEM((depth, rows, cols), jnp.bfloat16),
+    ] + [pltpu.SemaphoreType.DMA((tensors,))] * 2 + [pltpu.SemaphoreType.DMA((depth,))] * 4
+
+
+def gather_sems(tensors):
+    return [pltpu.SemaphoreType.DMA((tensors,))] * 6
+
+
+def scatter_sum(at, part, narrow, widen, scratch, total):
+    pair_out, pair_in, y_out, y_in, z_out, z_in = scratch[:6]
+    pair_send, pair_recv, y_send, y_recv, z_send, z_recv = scratch[6:]
+    depth, r = at.depth, at.r
 
     def pair(d):
-        return to_sibling(pair_out.at[d], pair_in.at[d], pair_send.at[d], pair_recv.at[d], r)
-
-    def ahead(d):
-        pair_out[d] = part(2 * d + 1 - r)
-        pair(d).start()
-
-    ahead(lax.rem(t + 1, tensors))
-
-    def step(k, _):
-        d = lax.rem(t + 1 + k, tensors)
-        ahead(lax.rem(t + 2 + k, tensors))
+        return remote(
+            pair_out.at[d], pair_in.at[d], pair_send.at[d], pair_recv.at[d], {"role": 1 - r}
+        )
+
+    def cross(z):
+        return remote(
+            y_out.at[z], y_in.at[z], y_send.at[z], y_recv.at[z], {"tensor": at.across(at.z)}
+        )
+
+    def line(z):
+        return remote(
+            z_out.at[z], z_in.at[at.z], z_send.at[z], z_recv.at[at.z], {"tensor": at.along(z)}
+        )
+
+    def arrived(z):
+        return remote(
+            z_out.at[z], z_in.at[z], z_send.at[z], z_recv.at[z], {"tensor": at.along(z)}
+        )
+
+    def dests(z):
+        return [at.across(z), at.along(z)] if at.lanes == 2 else [at.along(z)]
+
+    def first(k):
+        for d in dests(at.after(k)):
+            pair_out[d] = part(2 * d + 1 - r)
+            pair(d).start()
+
+    def second(k):
+        z = at.after(k)
+        if at.lanes == 2:
+            d = at.across(z)
+            own = part(2 * d + r)
+            pair(d).wait_recv()
+            y_out[z] = narrow(own + pair_in[d])
+            cross(z).start()
+        d = at.along(z)
         own = part(2 * d + r)
         pair(d).wait_recv()
-        out[d] = narrow(own + pair_in[d])
-        to_peer(out.at[d], inn.at[t], send.at[d], recv.at[t], d).start()
+        pair_in[d] = own + pair_in[d]
+
+    def merged(z):
+        value = pair_in[at.along(z)]
+        if at.lanes == 2:
+            cross(z).wait_recv()
+            value = value + widen(y_in[z])
+        return value
+
+    def third(k):
+        z = at.after(k)
+        z_out[z] = narrow(merged(z))
+        line(z).start()
+
+    first(1)
+    if depth > 2:
+        first(2)
+    second(1)
+
+    def step(k, _):
+        first(k + 1)
+        second(k)
+        third(k - 1)
         return 0
 
-    lax.fori_loop(0, tensors - 1, step, 0)
-    own = part(2 * t + r)
-    pair(t).wait_recv()
-    total[...] = own + pair_in[t]
+    lax.fori_loop(2, depth, step, 0)
+    if depth == 2:
+        first(depth)
+    second(depth)
+    third(depth - 1)
+    total[...] = merged(at.z)
 
     def collect(k, _):
-        s = lax.rem(t + tensors - k, tensors)
-        to_peer(out.at[s], inn.at[s], send.at[s], recv.at[s], s).wait_recv()
-        total[...] += inn[s].astype(jnp.float32)
+        z = at.before(k)
+        arrived(z).wait_recv()
+        total[...] += widen(z_in[z])
         return 0
 
-    lax.fori_loop(1, tensors, collect, 0)
+    lax.fori_loop(1, depth, collect, 0)
 
     def finish(k, _):
-        s = lax.rem(t + k, tensors)
-        to_peer(out.at[s], inn.at[t], send.at[s], recv.at[t], s).wait_send()
-        pair(s).wait_send()
+        z = at.after(k)
+        line(z).wait_send()
         return 0
 
-    lax.fori_loop(1, tensors, finish, 0)
-    pair(t).wait_send()
-
-
-def gather_blocks(tensors, t, r, buf, sems, use):
-    send, recv, pair_send, pair_recv = sems
-    mine = 2 * t + r
-
-    def spread(k, _):
-        d = lax.rem(t + k, tensors)
-        to_peer(buf.at[mine], buf.at[mine], send.at[d], recv.at[t], d).start()
+    lax.fori_loop(1, depth, finish, 0)
+
+    def finish_near(k, _):
+        z = at.after(k)
+        for d in dests(z):
+            pair(d).wait_send()
+        if at.lanes == 2:
+            cross(z).wait_send()
         return 0
 
-    lax.fori_loop(1, tensors, spread, 0)
-
-    def pair(s, q):
-        return to_sibling(buf.at[q], buf.at[q], pair_send.at[s], pair_recv.at[s], r)
-
-    pair(t, mine).start()
-    use(mine)
-
-    def near(k, _):
-        s = lax.rem(t + tensors - k, tensors)
-        q = 2 * s + r
-        to_peer(buf.at[q], buf.at[q], send.at[s], recv.at[s], s).wait_recv()
-        pair(s, q).start()
-        use(q)
-        return 0
-
-    lax.fori_loop(1, tensors, near, 0)
-
-    def far(k, _):
-        s = lax.rem(t + tensors - k, tensors)
-        q = 2 * s + 1 - r
-        pair(s, q).wait_recv()
-        use(q)
-        return 0
-
-    lax.fori_loop(0, tensors, far, 0)
-
-    def finish(k, _):
-        s = lax.rem(t + k, tensors)
-        to_peer(buf.at[mine], buf.at[mine], send.at[s], recv.at[t], s).wait_send()
-        pair(s, 2 * s + r).wait_send()
-        return 0
-
-    lax.fori_loop(1, tensors, finish, 0)
-    pair(t, mine).wait_send()
+    lax.fori_loop(0, depth, finish_near, 0)
+
+
+class Gather:
+    def __init__(self, at, buf, sems, use):
+        self.at, self.buf, self.sems, self.use = at, buf, sems, use
+
+    def line(self, z):
+        at, mine = self.at, self.buf.at[self.at.mine]
+        return remote(
+            mine, mine, self.sems[0].at[z], self.sems[1].at[at.z], {"tensor": at.along(z)}
+        )
+
+    def arrived(self, z):
+        at = self.at
+        block = self.buf.at[2 * at.along(z) + at.r]
+        return remote(
+            block, block, self.sems[0].at[z], self.sems[1].at[z], {"tensor": at.along(z)}
+        )
+
+    def cross(self, z, t):
+        at = self.at
+        block = self.buf.at[2 * t + at.r]
+        return remote(
+            block, block, self.sems[2].at[z], self.sems[3].at[z], {"tensor": at.across(at.z)}
+        )
+
+    def pair(self, t, r):
+        block = self.buf.at[2 * t + r]
+        return remote(
+            block, block, self.sems[4].at[t], self.sems[5].at[t], {"role": 1 - self.at.r}
+        )
+
+    def start(self):
+        at = self.at
+        if at.lanes == 2:
+            self.cross(at.z, at.t).start()
+
+        def spread(k, _):
+            self.line(at.after(k)).start()
+            return 0
+
+        lax.fori_loop(1, at.depth, spread, 0)
+        self.pair(at.t, at.r).start()
+
+    def over(self, k):
+        at = self.at
+        if at.lanes == 2:
+            z = at.before(k)
+            t = at.across(z)
+            self.cross(z, t).wait_recv()
+            self.pair(t, at.r).start()
+            self.use(2 * t + at.r)
+
+    def relay(self):
+        at = self.at
+        self.use(at.mine)
+
+        def step(k, _):
+            z = at.before(k)
+            t = at.along(z)
+            self.arrived(z).wait_recv()
+            if at.lanes == 2:
+                self.cross(z, t).start()
+            self.pair(t, at.r).start()
+            self.use(2 * t + at.r)
+            self.over(k - 1)
+            return 0
+
+        lax.fori_loop(1, at.depth, step, 0)
+        self.over(at.depth - 1)
+
+    def finish(self):
+        at = self.at
+
+        def far(k, _):
+            z = at.before(k)
+            for t in [at.along(z)] + ([at.across(z)] if at.lanes == 2 else []):
+                self.pair(t, 1 - at.r).wait_recv()
+                self.use(2 * t + 1 - at.r)
+            return 0
+
+        lax.fori_loop(0, at.depth, far, 0)
+
+        def sent(k, _):
+            z = at.after(k)
+            self.pair(at.along(z), at.r).wait_send()
+            if at.lanes == 2:
+                self.cross(z, at.along(z)).wait_send()
+                self.pair(at.across(z), at.r).wait_send()
+            return 0
+
+        lax.fori_loop(0, at.depth, sent, 0)
+
+        def line_sent(k, _):
+            self.line(at.after(k)).wait_send()
+            return 0
+
+        lax.fori_loop(1, at.depth, line_sent, 0)
 
 
 def front_kernel(
-    tensors, context, w_out, residual, fc_rest, w_fc, captured, features,
-    pair_out, pair_in, out, inn, total, cap_buf, feat_buf, *sems,
+    tensors, context, w_out, residual, fc_rest, w_fc, own_gain, captured, features, gain,
+    total, cap_buf, feat_buf, gain_buf, *scratch,
 ):
-    t, r = lax.axis_index("tensor"), lax.axis_index("role")
+    at = Place(tensors)
     cols = w_fc.shape[1]
-    mine = 2 * t + r
-    greet(tensors, t, r)
-
-    def part(q):
-        return product(context[...], w_out[:, pl.ds(pl.multiple_of(q * cols, cols), cols)])
-
-    scatter_sum(
-        tensors, t, r, part, lambda x: x.astype(jnp.bfloat16),
-        (pair_out, pair_in, out, inn), sems[:4], total,
-    )
-    cap_buf[mine] = (total[...] + residual[...].astype(jnp.float32)).astype(jnp.bfloat16)
-    total[...] = fc_rest[...].astype(jnp.float32)
+    gain_buf[at.mine] = jnp.broadcast_to(own_gain[...], gain_buf.shape[1:])
+    at.greet()
+
+    def span(q):
+        return pl.ds(pl.multiple_of(q * cols, cols), cols)
+
+    def keep_gain(q):
+        gain[:, span(q)] = gain_buf[q][:1]
 
     def multiply(q):
         block = cap_buf[q]
         captured[q] = block
-        total[...] += product(block, w_fc[pl.ds(pl.multiple_of(q * cols, cols), cols), :])
-
-    gather_blocks(tensors, t, r, cap_buf, sems[4:8], multiply)
-    feat_buf[mine] = total[...].astype(jnp.bfloat16)
+        total[...] += product(block, w_fc[span(q), :])
 
     def place(q):
-        features[:, pl.ds(pl.multiple_of(q * cols, cols), cols)] = feat_buf[q]
-
-    gather_blocks(tensors, t, r, feat_buf, sems[8:12], place)
-
-
-def front(tensors, context, w_out, residual, fc_rest, w_fc):
+        features[:, span(q)] = feat_buf[q]
+
+    gains = Gather(at, gain_buf, scratch[12:18], keep_gain)
+    caps = Gather(at, cap_buf, scratch[18:24], multiply)
+    feats = Gather(at, feat_buf, scratch[24:30], place)
+
+    gains.start()
+    scatter_sum(
+        at, lambda q: product(context[...], w_out[:, span(q)]), lambda x: x.astype(jnp.bfloat16),
+        lambda x: x.astype(jnp.float32), scratch[:12], total,
+    )
+    cap_buf[at.mine] = (total[...] + residual[...].astype(jnp.float32)).astype(jnp.bfloat16)
+    caps.start()
+    total[...] = fc_rest[...].astype(jnp.float32)
+    gains.relay()
+    caps.relay()
+    caps.finish()
+    feat_buf[at.mine] = total[...].astype(jnp.bfloat16)
+    feats.start()
+    gains.finish()
+    feats.relay()
+    feats.finish()
+
+
+def front(tensors, context, w_out, residual, fc_rest, w_fc, norm_gain):
     rows = context.shape[0]
     width, cols = w_fc.shape
     blocks = 2 * tensors
@@ -183,23 +341,22 @@
         out_shape=(
             jax.ShapeDtypeStruct((blocks, rows, cols), jnp.bfloat16),
             jax.ShapeDtypeStruct((rows, width), jnp.bfloat16),
+            jax.ShapeDtypeStruct((1, width), jnp.float32),
         ),
-        in_specs=[in_vmem()] * 5,
-        out_specs=(in_vmem(), in_vmem()),
+        in_specs=[in_vmem()] * 6,
+        out_specs=(in_vmem(), in_vmem(), in_vmem()),
         scratch_shapes=[
-            pltpu.VMEM((tensors, rows, cols), jnp.float32),
-            pltpu.VMEM((tensors, rows, cols), jnp.float32),
-            pltpu.VMEM((tensors, rows, cols), jnp.bfloat16),
-            pltpu.VMEM((tensors, rows, cols), jnp.bfloat16),
             pltpu.VMEM((rows, cols), jnp.float32),
             pltpu.VMEM((blocks, rows, cols), jnp.bfloat16),
             pltpu.VMEM((blocks, rows, cols), jnp.bfloat16),
+            pltpu.VMEM((blocks, 8, cols), jnp.float32),
         ]
-        + [pltpu.SemaphoreType.DMA((tensors,))] * 12,
+        + scatter_scratch(tensors, rows, cols)
+        + gather_sems(tensors) * 3,
         compiler_params=pltpu.CompilerParams(
             collective_id=0, has_side_effects=True, vmem_limit_bytes=VMEM_BYTES
         ),
-    )(context, w_out, residual, fc_rest, w_fc)
+    )(context, w_out, residual, fc_rest, w_fc, norm_gain[None, :])
 
 
 def stats_kernel(tensors, stats, summed, buf, send, recv):
@@ -261,19 +418,15 @@
     )(stats)
 
 
-def back_kernel(
-    tensors, dlogits, w_lm, scales, gain, features, summed, pair_out, pair_in, out, inn, *sems
-):
-    t, r = lax.axis_index("tensor"), lax.axis_index("role")
-    rows, cols = features.shape[0], out.shape[2]
-    greet(tensors, t, r)
+def back_kernel(tensors, dlogits, w_lm, scales, gain, features, summed, *scratch):
+    at = Place(tensors)
+    rows, cols = features.shape[0], summed.shape[1]
+    at.greet()
     line = lax.broadcasted_iota(jnp.int32, (EXTRA, cols), 0)
 
     def part(q):
         span = pl.ds(pl.multiple_of(q * cols, cols), cols)
-        grads = lax.dot_general(
-            dlogits[...], w_lm[span, :], (((1,), (1,)), ((), ())), preferred_element_type=jnp.float32
-        )
+        grads = product(dlogits[...], w_lm[:, span])
         one, two = grads[:rows], grads[rows:]
         level = gain[:, span]
         here = scales[:, 0:1] * one + scales[:, 1:2] * two
@@ -291,7 +444,12 @@
         tail = jnp.where(line == 0, high, jnp.where(line == 1, gain_row - high, 0.0))
         return jnp.concatenate([x[:rows], tail], axis=0).astype(jnp.bfloat16)
 
-    scatter_sum(tensors, t, r, part, narrow, (pair_out, pair_in, out, inn), sems, summed)
+    def widen(x):
+        wide = x.astype(jnp.float32)
+        gain_row = wide[rows : rows + 1] + wide[rows + 1 : rows + 2]
+        return jnp.concatenate([wide[:rows], jnp.where(line == 0, gain_row, 0.0)], axis=0)
+
+    scatter_sum(at, part, narrow, widen, scratch, summed)
 
 
 def back(tensors, dlogits, w_lm, scales, gain, features):
@@ -303,17 +461,11 @@
         out_shape=jax.ShapeDtypeStruct((tall, cols), jnp.float32),
         in_specs=[in_vmem()] * 5,
         out_specs=in_vmem(),
-        scratch_shapes=[
-            pltpu.VMEM((tensors, tall, cols), jnp.float32),
-            pltpu.VMEM((tensors, tall, cols), jnp.float32),
-            pltpu.VMEM((tensors, tall, cols), jnp.bfloat16),
-            pltpu.VMEM((tensors, tall, cols), jnp.bfloat16),
-        ]
-        + [pltpu.SemaphoreType.DMA((tensors,))] * 4,
+        scratch_shapes=scatter_scratch(tensors, tall, cols),
         compiler_params=pltpu.CompilerParams(
             collective_id=2, has_side_effects=True, vmem_limit_bytes=VMEM_BYTES
         ),
-    )(dlogits, w_lm, scales, gain, features)
+    )(dlogits, w_lm.T, scales, gain, features)
 
 
 def later_row(x):
@@ -333,7 +485,6 @@
     width, cols = w_fc.shape
     vocab_own = w_lm.shape[1]
 
-    gain = lax.all_gather(norm_gain, ("tensor", "role"), axis=0, tiled=True)[None, :]
     seg_now = segments[:rows]
     follows = jnp.concatenate(
         [
@@ -344,7 +495,7 @@
     labels_all = vocab_map[tokens]
     columns = position * vocab_own + jnp.arange(vocab_own, dtype=jnp.int32)
 
-    captured, features = front(tensors, context, w_out, residual, fc_rest, w_fc)
+    captured, features, gain = front(tensors, context, w_out, residual, fc_rest, w_fc, norm_gain)
 
     state = features.astype(jnp.float32)
     scale_one = lax.rsqrt(jnp.sum(state * state, axis=1) / width + EPS)
@@ -432,7 +583,7 @@
         - state_own * pull_one[:, None]
         - second_own * pull_two[:, None]
     ).astype(jnp.bfloat16)
-    grad_gain = summed[rows] + summed[rows + 1] - jnp.sum(pulled * state_own, axis=0)
+    grad_gain = summed[rows] - jnp.sum(pulled * state_own, axis=0)
     grad_fc = (
         jnp.einsum("pti,tj->pij", captured, gradient_sum, preferred_element_type=jnp.float32)
         .astype(jnp.bfloat16)

time: 253 us -> 178 us (0.70)
  the two profiles are of different devices: /device:TPU:15 before, /device:TPU:0 now
where the time goes in v2:
time: 178 us; the launch traced here: 177 us
  Pallas kernels  132 us (74%)
  other arithmetic  19 us (11%)
  matrix products  17.9 us (10%)
  local copies, waits for them, and re-layouts  5.26 us (3%)
  between operations  3.44 us (2%)
    pallas_call x1, Pallas kernels, front(): pl.pallas_call(functools.partial(front_kernel, tensors), out_shape=(jax.S...  85.9 us
    pallas_call x1, Pallas kernels, back(): pl.pallas_call(functools.partial(back_kernel, tensors), out_shape=jax.Sha...  35.5 us
    dot_general x1, matrix products, product(): return jnp.dot(a, b, preferred_element_type=jnp.float32)  10.9 us
    pallas_call x1, Pallas kernels, group_sum(): pl.pallas_call(functools.partial(stats_kernel, tensors), out_shape=jax.Sh...  10.2 us
    dot_general x1, matrix products, on_device(): jnp.einsum('pti,tj->pij', captured, gradient_sum, preferred_element_type=...  6.97 us

profile of v2, /device:TPU:0, one launch (start us, length us, event | category | flops | bytes accessed | tf_op | source)
XLA Modules:
  0.0 177.1 jit_solution(9071673341513580750)
XLA Ops:
  0.7 85.9 %shard_map.121 = (bf16[16,160,512]{2,1,0:T(8,128)(2,1)}, bf16[160,8192]{1,0:T(8,128)(2,1)}, f32[1,8192]{1,0:T(1,128)}) custom-call(bf16[160,512]{1,0:T(8,128)(2,1)} %context.1, bf16[512,8192]{1,0:T(8,128)(2,1)} %w_out.1, bf16[160,512]{1,0:T(8,128)(2,1)} %residual.1, bf16[160,512]{1,0:T(8,128)(2,1)} %fc_rest.1, bf16[8192,512]{1,0:T(8,128)(2,1)} %w_fc.1, ...), custom_call_target="tpu_custom_call" | custom-call | tf_op jit(solution)/shard_map/pallas_call | solution.py:339
  86.5 0.1 compare_convert_fusion.2
  86.6 0.1 pad_maximum_fusion.4
  86.7 2.5 %fusion = f32[160]{0:T(256)S(1)} fusion(bf16[160,8192]{1,0:T(8,128)(2,1)} %get-tuple-element.6.features), kind=kLoop, calls=%fused_computation.5 | loop fusion | flops 3932000 | bytes 2622080 | tf_op jit(solution)/shard_map/reduce_sum | solution.py:501
  89.2 2.5 %fusion.2 = bf16[160,8192]{1,0:T(8,128)(2,1)S(1)} fusion(bf16[160,8192]{1,0:T(8,128)(2,1)} %get-tuple-element.6.features, f32[8192]{0:T(1024)} %bitcast.38, f32[160]{0:T(256)S(1)} %add_rsqrt_fusion.1), kind=kLoop, calls=%fused_computation.7 | loop fusion | flops 5242880 | bytes 5276288 | tf_op jit(solution)/shard_map/convert_element_type | solution.py:502
  91.7 2.2 %multiply_reduce_fusion = (f32[160]{0:T(256)S(1)}, f32[160]{0:T(256)S(1)}) fusion(bf16[160,8192]{1,0:T(8,128)(2,1)S(1)} %copy-done.1, f32[160]{0:T(256)S(1)} %pad_maximum_fusion.4, bf16[159,8192]{1,0:T(8,128)(2,1)S(1)} %bitcast.33), kind=kLoop, calls=%fused_computation.12 | loop fusion | flops 10485440 | bytes 5228416 | tf_op jit(solution)/shard_map/reduce_sum | solution.py:507
  94.0 3.1 %multiply_convert_fusion = bf16[160,8192]{1,0:T(8,128)(2,1)} fusion(bf16[160,8192]{1,0:T(8,128)(2,1)S(1)} %copy-done.1, f32[160]{0:T(256)S(1)} %add_rsqrt_fusion, f32[160]{0:T(256)S(1)} %pad_maximum_fusion.4, f32[8192]{0:T(1024)S(1)} %bitcast.39, bf16[159,8192]{1,0:T(8,128)(2,1)S(1)} %bitcast.34), kind=kLoop, calls=%fused_computation.13 | loop fusion | flops 9175040 | bytes 7881984 | tf_op jit(solution)/shard_map/convert_element_type | solution.py:506
  97.1 10.9 %fusion.3 = f32[320,1000]{1,0:T(8,128)} fusion(bf16[8192,1000]{0,1:T(8,128)(2,1)} %param.16, bf16[160,8192]{1,0:T(8,128)(2,1)} %multiply_convert_fusion, bf16[160,8192]{1,0:T(8,128)(2,1)S(1)} %fusion.2), kind=kOutput, calls=%fused_computation.8 | convolution fusion | flops 5253365760 | bytes 22906880 | tf_op jit(solution)/shard_map/dot_general | solution.py:22
  108.1 1.6 gather_fusion
  109.7 0.1 fusion.38
  109.8 2.1 %fusion.12 = (f32[160]{0:T(256)S(1)}, f32[160]{0:T(256)S(1)}, f32[160]{0:T(256)S(1)}, f32[160]{0:T(256)S(1)}, f32[160]{0:T(256)S(1)}, /*index=5*/f32[160]{0:T(256)S(1)}, f32[160]{0:T(256)S(1)}, f32[160]{0:T(256)S(1)}) fusion(f32[320,1000]{1,0:T(8,128)} %fusion.3, s32[1000]{0:T(1024)S(1)} %iota_add_fusion, s32[160]{0:T(256)S(1)} %get-tuple-element.42, ...), kind=kLoop, calls=%fused_computation.26 | loop fusion | flops 2878720 | bytes 1290400 | tf_op jit(solution)/shard_map/reduce_sum | solution.py:522
  111.8 0.6 stack.50.stats
  112.4 10.2 %shard_map.122 = f32[8,160]{1,0:T(8,128)} custom-call(f32[8,160]{1,0:T(8,128)} %stack.50.stats), custom_call_target="tpu_custom_call" | custom-call | tf_op jit(solution)/shard_map/pallas_call | solution.py:405
  122.6 1.0 fusion.37
  123.6 0.1 subtract_multiply_fusion.1
  123.7 0.6 subtract_multiply_fusion
  125.6 0.1 slice.63
  125.7 0.1 fusion.30
  125.8 0.6 convert_reduce_fusion.1
  127.7 0.6 pad_maximum_fusion.5
  128.3 0.9 constant_dynamic-slice_fusion
  129.2 0.1 convert_add_fusion.1
  129.3 1.7 fusion.10
  131.0 0.9 pad_maximum_fusion.dlogits
  132.0 0.1 fusion.28
  132.1 0.8 copy.18.scales
  132.8 35.5 %shard_map.123 = f32[176,512]{1,0:T(8,128)} custom-call(bf16[320,1000]{1,0:T(8,128)(2,1)} %pad_maximum_fusion.dlogits, bf16[1000,8192]{1,0:T(8,128)(2,1)} %bitcast.35, f32[160,3]{1,0:T(8,128)} %copy.18.scales, f32[1,8192]{1,0:T(1,128)} %get-tuple-element.7.gain, bf16[160,8192]{1,0:T(8,128)(2,1)} %get-tuple-element.6.features), custom_call_target="tpu_custom_call" | custom-call | tf_op jit(solution)/shard_map/pallas_call | solution.py:459
  168.3 0.1 slice.71
  168.4 0.1 slice_multiply_fusion
  168.5 7.0 %convolution_convert_fusion = bf16[16,512,512]{2,1,0:T(8,128)(2,1)} fusion(bf16[16,160,512]{2,1,0:T(8,128)(2,1)S(1)} %copy-done.3, f32[160,512]{1,0:T(8,128)S(1)} %convert_add_fusion.1, f32[176,512]{1,0:T(8,128)} %shard_map.123, f32[159,512]{1,0:T(8,128)S(1)} %slice_multiply_fusion, f32[160]{0:T(256)S(1)} %get-tuple-element.26, ...), kind=kOutput, calls=%fused_computation.4 | convolution fusion | flops 1347108864 | bytes 12158852 | tf_op jit(solution)/shard_map/pti,tj->pij/dot_general | solution.py:588
  175.5 1.0 fusion.20
  176.6 0.6 sub.51
  (26 shorter events, 0.2 us)
Async XLA Ops:
  0.6 107.4 %copy-start = (s32[128256]{0:T(1024)S(1)}, s32[128256]{0:T(1024)}, u32[]{:S(2)}) copy-start(s32[128256]{0:T(1024)} %param.19) | copy-start | bytes 1539076
  0.6 85.9 %copy-start.5 = (s32[162]{0:T(256)S(1)}, s32[162]{0:T(256)}, u32[]{:S(2)}) copy-start(s32[162]{0:T(256)} %param.18) | copy-start | bytes 1948
  86.5 5.2 %copy-start.1 = (bf16[160,8192]{1,0:T(8,128)(2,1)S(1)}, bf16[160,8192]{1,0:T(8,128)(2,1)}, u32[]{:S(2)}) copy-start(bf16[160,8192]{1,0:T(8,128)(2,1)} %get-tuple-element.6.features) | copy-start | bytes 7864324
  89.2 4.8 %copy-start.4 = (f32[1,8192]{1,0:T(1,128)S(1)}, f32[1,8192]{1,0:T(1,128)}, u32[]{:S(2)}) copy-start(f32[1,8192]{1,0:T(1,128)} %get-tuple-element.7.gain) | copy-start | bytes 98308
  91.7 5.4 %copy-start.2 = (bf16[160,8192]{1,0:T(8,128)(2,1)}, bf16[160,8192]{1,0:T(8,128)(2,1)S(1)}, u32[]{:S(2)}) copy-start(bf16[160,8192]{1,0:T(8,128)(2,1)S(1)} %fusion.2) | copy-start | bytes 7864324
  97.1 10.9 %copy-start.7 = (s32[162]{0:T(256)S(1)}, s32[162]{0:T(256)}, u32[]{:S(2)}) copy-start(s32[162]{0:T(256)} %param.17) | copy-start | bytes 1948
  132.8 35.7 %copy-start.3 = (bf16[16,160,512]{2,1,0:T(8,128)(2,1)S(1)}, bf16[16,160,512]{2,1,0:T(8,128)(2,1)}, u32[]{:S(2)}) copy-start(bf16[16,160,512]{2,1,0:T(8,128)(2,1)} %get-tuple-element.8) | copy-start | bytes 7864324
  132.8 35.7 %copy-start.6 = (f32[512]{0:T(512)S(1)}, f32[512]{0:T(512)}, u32[]{:S(2)}) copy-start(f32[512]{0:T(512)} %param.15) | copy-start | bytes 6148
  168.5 8.0 %slice-start = ((f32[176,512]{1,0:T(8,128)}), f32[1,512]{1,0:T(1,128)S(1)}, s32[]{:S(2)}) async-start(f32[176,512]{1,0:T(8,128)} %shard_map.123), calls=%async_computation | async-start | bytes 4096 | tf_op jit(solution)/shard_map/slice | solution.py:586

commit v3 on v2

v3 whole, which is shorter than its diff:
```python
import functools

import jax
import jax.numpy as jnp
from jax import lax
from jax.experimental import pallas as pl
from jax.experimental.pallas import tpu as pltpu
from jax.sharding import PartitionSpec as P

EPS = 1e-05
SHRINK = 1.0 / 1024.0
VMEM_BYTES = 60 * 1024 * 1024
EXTRA = 16
LANES = 128
MESH = pl.DeviceIdType.MESH


def in_vmem():
    return pl.BlockSpec(memory_space=pltpu.VMEM)


def product(a, b):
    return jnp.dot(a, b, preferred_element_type=jnp.float32)


class Place:
    def __init__(self, tensors):
        self.lanes = 2 if tensors == 8 else 1
        self.depth = tensors // self.lanes
        self.tensors = tensors
        self.t, self.r = lax.axis_index("tensor"), lax.axis_index("role")
        self.z, self.y = self.t // self.lanes, lax.rem(self.t, self.lanes)
        self.mine = 2 * self.t + self.r

    def before(self, k):
        return lax.rem(self.z + self.depth - k, self.depth)

    def after(self, k):
        return lax.rem(self.z + k, self.depth)

    def across(self, z):
        return z * 2 + 1 - self.y

    def along(self, z):
        return z * self.lanes + self.y

    def other(self, k):
        q = lax.rem(self.mine + k, 2 * self.tensors)
        return q, {"tensor": q // 2, "role": lax.rem(q, 2)}

    def greet(self):
        barrier = pltpu.get_barrier_semaphore()
        others = 2 * self.tensors

        def hello(k, _):
            pl.semaphore_signal(barrier, inc=1, device_id=self.other(k)[1], device_id_type=MESH)
            return 0

        lax.fori_loop(1, others, hello, 0)
        pl.semaphore_wait(barrier, others - 1)


def remote(src, dst, send_sem, recv_sem, target):
    return pltpu.make_async_remote_copy(
        src_ref=src, dst_ref=dst, send_sem=send_sem, recv_sem=recv_sem,
        device_id=target, device_id_type=MESH,
    )


def scatter_scratch(tensors, rows, cols):
    depth = tensors // (2 if tensors == 8 else 1)
    return [pltpu.VMEM((tensors, rows, cols), jnp.float32)] * 2 + [
        pltpu.VMEM((depth, rows, cols), jnp.bfloat16)
    ] * 4


def scatter_sems(tensors):
    depth = tensors // (2 if tensors == 8 else 1)
    return [pltpu.SemaphoreType.DMA((tensors,))] * 2 + [pltpu.SemaphoreType.DMA((depth,))] * 4


def gather_sems(tensors):
    return [pltpu.SemaphoreType.DMA((tensors,))] * 6


def scatter_sum(at, part, narrow, widen, buffers, sems, total):
    height = total.shape[0]
    pair_out, pair_in, y_out, y_in, z_out, z_in = [b.at[:, pl.ds(0, height), :] for b in buffers]
    pair_send, pair_recv, y_send, y_recv, z_send, z_recv = sems
    depth, r = at.depth, at.r

    def pair(d):
        return remote(
            pair_out.at[d], pair_in.at[d], pair_send.at[d], pair_recv.at[d], {"role": 1 - r}
        )

    def cross(z):
        return remote(
            y_out.at[z], y_in.at[z], y_send.at[z], y_recv.at[z], {"tensor": at.across(at.z)}
        )

    def line(z):
        return remote(
            z_out.at[z], z_in.at[at.z], z_send.at[z], z_recv.at[at.z], {"tensor": at.along(z)}
        )

    def arrived(z):
        return remote(
            z_out.at[z], z_in.at[z], z_send.at[z], z_recv.at[z], {"tensor": at.along(z)}
        )

    def dests(z):
        return [at.across(z), at.along(z)] if at.lanes == 2 else [at.along(z)]

    def first(k):
        for d in dests(at.after(k)):
            pair_out[d] = part(2 * d + 1 - r)
            pair(d).start()

    def second(k):
        z = at.after(k)
        if at.lanes == 2:
            d = at.across(z)
            own = part(2 * d + r)
            pair(d).wait_recv()
            y_out[z] = narrow(own + pair_in[d])
            cross(z).start()
        d = at.along(z)
        own = part(2 * d + r)
        pair(d).wait_recv()
        pair_in[d] = own + pair_in[d]

    def merged(z):
        value = pair_in[at.along(z)]
        if at.lanes == 2:
            cross(z).wait_recv()
            value = value + widen(y_in[z])
        return value

    def third(k):
        z = at.after(k)
        z_out[z] = narrow(merged(z))
        line(z).start()

    first(1)
    if depth > 2:
        first(2)
    second(1)

    def step(k, _):
        first(k + 1)
        second(k)
        third(k - 1)
        return 0

    lax.fori_loop(2, depth, step, 0)
    if depth == 2:
        first(depth)
    second(depth)
    third(depth - 1)
    total[...] = merged(at.z)

    def collect(k, _):
        z = at.before(k)
        arrived(z).wait_recv()
        total[...] += widen(z_in[z])
        return 0

    lax.fori_loop(1, depth, collect, 0)

    def finish(k, _):
        z = at.after(k)
        line(z).wait_send()
        return 0

    lax.fori_loop(1, depth, finish, 0)

    def finish_near(k, _):
        z = at.after(k)
        for d in dests(z):
            pair(d).wait_send()
        if at.lanes == 2:
            cross(z).wait_send()
        return 0

    lax.fori_loop(0, depth, finish_near, 0)


class Gather:
    def __init__(self, at, buf, sems, use):
        self.at, self.buf, self.sems, self.use = at, buf, sems, use

    def line(self, z):
        at, mine = self.at, self.buf.at[self.at.mine]
        return remote(
            mine, mine, self.sems[0].at[z], self.sems[1].at[at.z], {"tensor": at.along(z)}
        )

    def arrived(self, z):
        at = self.at
        block = self.buf.at[2 * at.along(z) + at.r]
        return remote(
            block, block, self.sems[0].at[z], self.sems[1].at[z], {"tensor": at.along(z)}
        )

    def cross(self, z, t):
        at = self.at
        block = self.buf.at[2 * t + at.r]
        return remote(
            block, block, self.sems[2].at[z], self.sems[3].at[z], {"tensor": at.across(at.z)}
        )

    def pair(self, t, r):
        block = self.buf.at[2 * t + r]
        return remote(
            block, block, self.sems[4].at[t], self.sems[5].at[t], {"role": 1 - self.at.r}
        )

    def start(self):
        at = self.at
        if at.lanes == 2:
            self.cross(at.z, at.t).start()

        def spread(k, _):
            self.line(at.after(k)).start()
            return 0

        lax.fori_loop(1, at.depth, spread, 0)
        self.pair(at.t, at.r).start()

    def over(self, k):
        at = self.at
        if at.lanes == 2:
            z = at.before(k)
            t = at.across(z)
            self.cross(z, t).wait_recv()
            self.pair(t, at.r).start()
            self.use(2 * t + at.r)

    def relay(self):
        at = self.at
        self.use(at.mine)

        def step(k, _):
            z = at.before(k)
            t = at.along(z)
            self.arrived(z).wait_recv()
            if at.lanes == 2:
                self.cross(z, t).start()
            self.pair(t, at.r).start()
            self.use(2 * t + at.r)
            self.over(k - 1)
            return 0

        lax.fori_loop(1, at.depth, step, 0)
        self.over(at.depth - 1)

    def finish(self):
        at = self.at

        def far(k, _):
            z = at.before(k)
            for t in [at.along(z)] + ([at.across(z)] if at.lanes == 2 else []):
                self.pair(t, 1 - at.r).wait_recv()
                self.use(2 * t + 1 - at.r)
            return 0

        lax.fori_loop(0, at.depth, far, 0)

        def sent(k, _):
            z = at.after(k)
            self.pair(at.along(z), at.r).wait_send()
            if at.lanes == 2:
                self.cross(z, at.along(z)).wait_send()
                self.pair(at.across(z), at.r).wait_send()
            return 0

        lax.fori_loop(0, at.depth, sent, 0)

        def line_sent(k, _):
            self.line(at.after(k)).wait_send()
            return 0

        lax.fori_loop(1, at.depth, line_sent, 0)


def fold(x):
    total = x[:, :LANES]
    for start in range(LANES, x.shape[1], LANES):
        total = total + x[:, start : start + LANES]
    return total


def spread_sum(x):
    return jnp.broadcast_to(jnp.sum(x, axis=1, keepdims=True), x.shape)


def earlier(x):
    return pltpu.roll(x, 1, 0)


def later(x):
    return pltpu.roll(x, x.shape[0] - 1, 0)


def narrow_plain(x):
    return x.astype(jnp.bfloat16)


def widen_plain(x):
    return x.astype(jnp.float32)


def step_kernel(
    tensors, context, w_out, residual, fc_rest, own_gain, marks, flags, w_fc_far, w_lm_far,
    captured, grad_state, grad_gain, losses,
    w_fc, w_lm, total, cap_buf, feat_buf, gain_buf, moments, logits, dlogits, stats, shared,
    summed, load, *scratch,
):
    at = Place(tensors)
    rows, cols = context.shape[0], w_fc.shape[1]
    width, vocab_own = w_fc.shape[0], w_lm.shape[0]
    blocks = 2 * tensors
    buffers, sems = scratch[:6], scratch[6:]
    load_fc = pltpu.make_async_copy(w_fc_far, w_fc, load.at[0])
    load_lm = pltpu.make_async_copy(w_lm_far, w_lm, load.at[1])
    load_fc.start()
    load_lm.start()
    gain_buf[at.mine] = jnp.broadcast_to(own_gain[...], gain_buf.shape[1:])
    at.greet()

    def span(q):
        return pl.ds(pl.multiple_of(q * cols, cols), cols)

    def level(q):
        return gain_buf[q][:1]

    def multiply(q):
        block = cap_buf[q]
        captured[q] = block
        total[...] += product(block, w_fc[span(q), :])

    def head(q):
        state = feat_buf[q].astype(jnp.float32)
        scaled = state * level(q)
        before = earlier(scaled)
        moments[0] += fold(state * state)
        moments[1] += fold(state * before)
        moments[2] += fold(before * before)
        both = jnp.concatenate([scaled, before * level(q)], axis=0).astype(jnp.bfloat16)
        logits[...] += lax.dot_general(
            both, w_lm[:, span(q)], (((1,), (1,)), ((), ())), preferred_element_type=jnp.float32
        )

    gains = Gather(at, gain_buf, sems[0:6], lambda q: None)
    caps = Gather(at, cap_buf, sems[6:12], multiply)
    feats = Gather(at, feat_buf, sems[12:18], head)

    gains.start()
    scatter_sum(
        at, lambda q: product(context[...], w_out[:, span(q)]), narrow_plain, widen_plain,
        buffers, sems[18:24], total,
    )
    cap_buf[at.mine] = (total[...] + residual[...].astype(jnp.float32)).astype(jnp.bfloat16)
    caps.start()
    total[...] = fc_rest[...].astype(jnp.float32)
    moments[...] = jnp.zeros_like(moments)
    logits[...] = jnp.zeros_like(logits)
    gains.relay()
    load_fc.wait()
    caps.relay()
    caps.finish()
    feat_buf[at.mine] = total[...].astype(jnp.bfloat16)
    feats.start()
    gains.finish()
    load_lm.wait()
    feats.relay()
    feats.finish()

    follows = jnp.broadcast_to(flags[:, 0:1], (rows, LANES))
    usable_one, usable_two = flags[:, 1:2], flags[:, 2:3]
    squares, mixed, squares_before = [spread_sum(moments[i]) / width for i in range(3)]
    scale_one = lax.rsqrt(squares + EPS)
    link = follows * earlier(scale_one)
    cross = link * (mixed + link * squares_before)
    scale_two = lax.rsqrt(jnp.maximum(squares + link * mixed + cross, 0.0) + EPS)

    logits_one = logits[:rows] * scale_one[:, :1]
    logits_two = (logits[:rows] + logits[rows:] * link[:, :1]) * scale_two[:, :1]
    powers_one, powers_two = jnp.exp(logits_one), jnp.exp(logits_two)
    logits[:rows] = powers_one
    logits[rows:] = powers_two
    columns = lax.broadcasted_iota(jnp.int32, (rows, vocab_own), 1) + at.mine * vocab_own

    def matches(i):
        return columns == marks[:, i : i + 1]

    parts = [
        powers_one,
        powers_two,
        powers_one * (logits_one * SHRINK),
        powers_two * (logits_two * SHRINK),
        powers_two * (logits_one * SHRINK),
        jnp.where(matches(0), logits_one, 0.0),
        jnp.where(matches(1), logits_two, 0.0),
        jnp.where(matches(1), logits_one, 0.0),
    ]
    lane = lax.broadcasted_iota(jnp.int32, (rows, LANES), 1)
    packed = jnp.zeros((rows, LANES), jnp.float32)
    for i, values in enumerate(parts):
        packed = jnp.where(lane == i, jnp.sum(values, axis=1, keepdims=True), packed)
    tall = stats.shape[1]
    packed = jnp.concatenate([packed, jnp.zeros((tall - rows, LANES), jnp.float32)], axis=0)
    stats[...] = packed.T[: stats.shape[0]]
    shared[at.mine] = stats[...]

    def share(k):
        q, target = at.other(k)
        return remote(stats, shared.at[at.mine], sems[30].at[q], sems[31].at[at.mine], target)

    def spread(k, _):
        share(k).start()
        return 0

    lax.fori_loop(1, blocks, spread, 0)

    def collect(k, _):
        q, target = at.other(k)
        remote(stats, shared.at[q], sems[30].at[q], sems[31].at[q], target).wait_recv()
        share(k).wait_send()
        return 0

    lax.fori_loop(1, blocks, collect, 0)
    table = jnp.sum(shared[...], axis=0)
    table = jnp.concatenate([table, jnp.zeros((LANES - table.shape[0], tall), jnp.float32)], axis=0)
    table = table.T[:rows]
    (totals_one, totals_two, mean_one, mean_two, mean_mixed, picked_one, picked_two, picked_mixed) = [
        table[:, i : i + 1] for i in range(8)
    ]

    weight_one, weight_two = usable_one, 0.8 * usable_two

    def gradient(powers, totals, i, weight):
        return (weight * (powers / totals - matches(i).astype(jnp.float32))).astype(jnp.bfloat16)

    dlogits[:rows] = gradient(logits[:rows], totals_one, 0, weight_one)
    dlogits[rows:] = gradient(logits[rows:], totals_two, 1, weight_two)
    link_back = later(link * scale_two)
    line = lax.broadcasted_iota(jnp.int32, (EXTRA, cols), 0)

    def part(q):
        grads = product(dlogits[...], w_lm[:, span(q)])
        one, two = grads[:rows], grads[rows:]
        here = scale_one[:, :1] * one + scale_two[:, :1] * two
        ahead = link_back[:, :1] * later(two) * level(q)
        gain_part = jnp.sum(
            feat_buf[q].astype(jnp.float32) * (here + 2.0 * ahead), axis=0, keepdims=True
        )
        return jnp.concatenate(
            [level(q) * (here + ahead), jnp.where(line == 0, gain_part, 0.0)], axis=0
        )

    def narrow(x):
        gain_row = x[rows : rows + 1]
        high = gain_row.astype(jnp.bfloat16).astype(jnp.float32)
        tail = jnp.where(line == 0, high, jnp.where(line == 1, gain_row - high, 0.0))
        return jnp.concatenate([x[:rows], tail], axis=0).astype(jnp.bfloat16)

    def widen(x):
        wide = x.astype(jnp.float32)
        gain_row = wide[rows : rows + 1] + wide[rows + 1 : rows + 2]
        return jnp.concatenate([wide[:rows], jnp.where(line == 0, gain_row, 0.0)], axis=0)

    scatter_sum(at, part, narrow, widen, buffers, sems[24:30], summed)

    def average(totals, picked, usable):
        count = jnp.sum(usable, axis=0, keepdims=True)
        return jnp.sum(usable * (jnp.log(totals) - picked), axis=0, keepdims=True) / jnp.maximum(
            count, 1.0
        )

    row = lax.broadcasted_iota(jnp.int32, losses.shape, 1)
    losses[...] = jnp.where(
        row == 0,
        average(totals_one, picked_one, usable_one),
        average(totals_two, picked_two, usable_two),
    )

    def wide(x):
        return jnp.broadcast_to(x, (rows, LANES))

    dot_one = wide(weight_one * (mean_one / (SHRINK * totals_one) - picked_one))
    dot_two = wide(weight_two * (mean_two / (SHRINK * totals_two) - picked_two))
    dot_mixed = wide(weight_two * (mean_mixed / (SHRINK * totals_two) - picked_mixed))
    pull_two = scale_two**3 * (dot_two / (scale_two * width))
    back_link = follows * (dot_two / scale_two - dot_mixed / scale_one) / width
    through = later(follows * (scale_two * back_link - pull_two * cross))
    pull_one = scale_one**3 * ((dot_one / width + through) / scale_one)

    gain = own_gain[...]
    state = feat_buf[at.mine].astype(jnp.float32)
    second = state + link[:, :1] * earlier(state * gain)
    pulled = later(second * (follows * pull_two)[:, :1]) * scale_one[:, :1]
    grad_state[...] = (
        summed[:rows] - gain * pulled - state * pull_one[:, :1] - second * pull_two[:, :1]
    ).astype(jnp.bfloat16)
    grad_gain[...] = summed[rows : rows + 1] - jnp.sum(pulled * state, axis=0, keepdims=True)


def whole_step(tensors, context, w_out, residual, fc_rest, w_fc, norm_gain, w_lm, marks, flags):
    rows = context.shape[0]
    width, cols = w_fc.shape
    vocab_own = w_lm.shape[1]
    blocks = 2 * tensors
    tall = -(-rows // LANES) * LANES
    far = pl.BlockSpec(memory_space=pl.ANY)
    return pl.pallas_call(
        functools.partial(step_kernel, tensors),
        out_shape=(
            jax.ShapeDtypeStruct((blocks, rows, cols), jnp.bfloat16),
            jax.ShapeDtypeStruct((rows, cols), jnp.bfloat16),
            jax.ShapeDtypeStruct((1, cols), jnp.float32),
            jax.ShapeDtypeStruct((1, LANES), jnp.float32),
        ),
        in_specs=[in_vmem()] * 7 + [far] * 2,
        out_specs=(in_vmem(),) * 4,
        scratch_shapes=[
            pltpu.VMEM((width, cols), jnp.bfloat16),
            pltpu.VMEM((vocab_own, width), jnp.bfloat16),
            pltpu.VMEM((rows, cols), jnp.float32),
            pltpu.VMEM((blocks, rows, cols), jnp.bfloat16),
            pltpu.VMEM((blocks, rows, cols), jnp.bfloat16),
            pltpu.VMEM((blocks, 8, cols), jnp.float32),
            pltpu.VMEM((3, rows, LANES), jnp.float32),
            pltpu.VMEM((2 * rows, vocab_own), jnp.float32),
            pltpu.VMEM((2 * rows, vocab_own), jnp.bfloat16),
            pltpu.VMEM((8, tall), jnp.float32),
            pltpu.VMEM((blocks, 8, tall), jnp.float32),
            pltpu.VMEM((rows + EXTRA, cols), jnp.float32),
            pltpu.SemaphoreType.DMA((2,)),
        ]
        + scatter_scratch(tensors, rows + EXTRA, cols)
        + gather_sems(tensors) * 3
        + scatter_sems(tensors) * 2
        + [pltpu.SemaphoreType.DMA((blocks,))] * 2,
        compiler_params=pltpu.CompilerParams(
            collective_id=0, has_side_effects=True, vmem_limit_bytes=VMEM_BYTES
        ),
    )(context, w_out, residual, fc_rest, norm_gain[None, :], marks, flags, w_fc, w_lm.T)


def on_device(
    context, w_out, residual, fc_rest, w_fc, norm_gain, w_lm, tokens, segments, vocab_map
):
    tensors = lax.axis_size("tensor")
    rows = tokens.shape[0] - 2
    width, cols = w_fc.shape
    seg_now = segments[:rows]
    follows = jnp.concatenate(
        [
            jnp.zeros((1,), jnp.float32),
            (segments[1:rows] == segments[: rows - 1]).astype(jnp.float32),
        ]
    )
    labels_all = vocab_map[tokens]
    labels = [labels_all[shift : shift + rows] for shift in (1, 2)]
    usable = [
        ((labels[k - 1] >= 0) & (segments[k : k + rows] == seg_now)).astype(jnp.float32)
        for k in (1, 2)
    ]
    captured, grad_state, grad_gain, losses = whole_step(
        tensors, context, w_out, residual, fc_rest, w_fc, norm_gain, w_lm,
        jnp.stack(labels, axis=1), jnp.stack([follows] + usable, axis=1),
    )
    grad_fc = (
        jnp.einsum("pti,tj->pij", captured, grad_state, preferred_element_type=jnp.float32)
        .astype(jnp.bfloat16)
        .reshape(width, cols)
    )
    return (losses[0, :2], grad_fc, grad_gain[0])


def solution(mesh):
    placed = (
        P("groups", ("tensor", "role")),
        P(("tensor", "role"), None),
        P("groups", ("tensor", "role")),
        P("groups", ("tensor", "role")),
        P(None, ("tensor", "role")),
        P(("tensor", "role")),
        P(None, ("tensor", "role")),
        P("groups"),
        P("groups"),
        P("groups"),
    )
    return jax.shard_map(
        on_device,
        mesh=mesh,
        in_specs=placed,
        out_specs=(P("groups"), P("groups", ("tensor", "role")), P(("groups", "tensor", "role"))),
        check_vma=False,
    )
```

time: 178 us -> 133 us (0.75)
  other arithmetic: 19 us -> 2.49 us
  Pallas kernels: 132 us -> 117 us
  matrix products: 17.9 us -> 7.52 us
  between operations: 3.44 us -> 0.68 us
    pallas_call x3 -> x1, Pallas kernels: 132 us -> 117 us  [whole_step(): pl.pallas_call(functools.partial(step_kernel, tensors), out_shape=(jax.Sh...]
    dot_general x2 -> x1, matrix products: 17.9 us -> 7.52 us  [on_device(): jnp.einsum('pti,tj->pij', captured, grad_state, preferred_element_type=jn...]
    reduce_sum x5 -> x0, other arithmetic: 8.45 us -> none  [the longest x1 2.5 us: on_device(): scale_one = lax.rsqrt(jnp.sum(state * state, axis=1) / width + EPS)]
    convert_element_type x5 -> x0, other arithmetic: 7.34 us -> none  [the longest x1 3.13 us: on_device(): normed_two = (second * scale_two[:, None] * gain).astype(jnp.bfloat16)]
where the time goes in v3:
time: 133 us
  Pallas kernels  117 us (88%)
  matrix products  7.52 us (6%)
  local copies, waits for them, and re-layouts  4.76 us (4%)
  other arithmetic  2.49 us (2%)
    pallas_call x1, Pallas kernels, whole_step(): pl.pallas_call(functools.partial(step_kernel, tensors), out_shape=(jax.Sh...  117 us
    dot_general x1, matrix products, on_device(): jnp.einsum('pti,tj->pij', captured, grad_state, preferred_element_type=jn...  7.52 us

profile of v3, /device:TPU:0, one launch (start us, length us, event | category | flops | bytes accessed | tf_op | source)
XLA Modules:
  0.0 132.9 jit_solution(367893350011498250)
XLA Ops:
  0.6 0.0 copy-start
  0.6 0.8 slice_compare_fusion
  1.5 0.1 pad_add_fusion.1
  1.6 0.7 compare_select_fusion
  2.3 0.0 copy-done
  2.3 1.4 %gather_fusion = s32[162]{0:T(256)S(1)} fusion(s32[128256]{0:T(1024)S(1)} %copy-done, s32[1024]{0:T(1024)S(1)} %pad_clamp_fusion), kind=kCustom, calls=%fused_computation | custom fusion | bytes 1944 | tf_op jit(solution)/shard_map/gather | solution.py:565
  3.7 0.9 compare_and_fusion.1
  4.6 0.1 fusion.1
  4.7 0.7 copy.21.flags
  5.4 0.8 copy.20.marks
  6.2 117.5 %shard_map.121 = (bf16[16,160,512]{2,1,0:T(8,128)(2,1)}, bf16[160,512]{1,0:T(8,128)(2,1)}, f32[1,512]{1,0:T(1,128)}, f32[1,128]{1,0:T(1,128)}) custom-call(bf16[160,512]{1,0:T(8,128)(2,1)} %context.1, bf16[512,8192]{1,0:T(8,128)(2,1)} %w_out.1, bf16[160,512]{1,0:T(8,128)(2,1)} %residual.1, bf16[160,512]{1,0:T(8,128)(2,1)} %fc_rest.1, f32[1,512]{1,0:T(1,128)} %bitcast.16, ...), custom_call_target="tpu_custom_call" | custom-call | tf_op jit(solution)/shard_map/pallas_call | solution.py:517
  123.7 0.0 copy-start.1
  123.7 1.1 slice_bitcast_fusion
  124.8 7.5 %convolution_convert_fusion = bf16[16,512,512]{2,1,0:T(8,128)(2,1)} fusion(bf16[16,160,512]{2,1,0:T(8,128)(2,1)} %get-tuple-element.8, bf16[160,512]{1,0:T(8,128)(2,1)} %get-tuple-element.9), kind=kOutput, calls=%fused_computation.1 | convolution fusion | flops 1346371584 | bytes 11173888 | tf_op jit(solution)/shard_map/pti,tj->pij/dot_general | solution.py:576
  132.3 0.0 copy-done.1
  132.3 0.6 copy.23
  (6 shorter events, 0.1 us)
Async XLA Ops:
  0.6 1.6 %copy-start = (s32[128256]{0:T(1024)S(1)}, s32[128256]{0:T(1024)}, u32[]{:S(2)}) copy-start(s32[128256]{0:T(1024)} %param.19) | copy-start | bytes 1539076
  123.7 8.7 %copy-start.1 = (f32[1,512]{1,0:T(1,128)S(1)}, f32[1,512]{1,0:T(1,128)}, u32[]{:S(2)}) copy-start(f32[1,512]{1,0:T(1,128)} %get-tuple-element.10) | copy-start | bytes 6148

commit v4 on v3

--- a/solution.py
+++ b/solution.py
@@ -173,8 +173,6 @@
         line(z).wait_send()
         return 0
 
-    lax.fori_loop(1, depth, finish, 0)
-
     def finish_near(k, _):
         z = at.after(k)
         for d in dests(z):
@@ -183,7 +181,11 @@
             cross(z).wait_send()
         return 0
 
-    lax.fori_loop(0, depth, finish_near, 0)
+    def drain():
+        lax.fori_loop(1, depth, finish, 0)
+        lax.fori_loop(0, depth, finish_near, 0)
+
+    return drain
 
 
 class Gather:
@@ -267,6 +269,9 @@
 
         lax.fori_loop(0, at.depth, far, 0)
 
+    def drain(self):
+        at = self.at
+
         def sent(k, _):
             z = at.after(k)
             self.pair(at.along(z), at.r).wait_send()
@@ -312,10 +317,10 @@
 
 
 def step_kernel(
-    tensors, context, w_out, residual, fc_rest, own_gain, marks, flags, w_fc_far, w_lm_far,
+    tensors, context, residual, fc_rest, own_gain, labels, segments, w_out_far, w_fc_far, w_lm_far,
     captured, grad_state, grad_gain, losses,
-    w_fc, w_lm, total, cap_buf, feat_buf, gain_buf, moments, logits, dlogits, stats, shared,
-    summed, load, *scratch,
+    w_out, w_fc, w_lm, total, cap_buf, feat_buf, gain_buf, moments, logits, dlogits, stats, shared,
+    summed, notes, load, load_out, *scratch,
 ):
     at = Place(tensors)
     rows, cols = context.shape[0], w_fc.shape[1]
@@ -324,21 +329,35 @@
     buffers, sems = scratch[:6], scratch[6:]
     load_fc = pltpu.make_async_copy(w_fc_far, w_fc, load.at[0])
     load_lm = pltpu.make_async_copy(w_lm_far, w_lm, load.at[1])
+
+    def span(q):
+        return pl.ds(pl.multiple_of(q * cols, cols), cols)
+
+    def out_block(q):
+        return pltpu.make_async_copy(
+            w_out_far.at[:, span(q)], w_out.at[:, span(q)], load_out.at[q]
+        )
+
+    def fetch(k, _):
+        z = at.after(k)
+        order = [at.across(z), at.along(z)] if at.lanes == 2 else [at.along(z)]
+        for d in order:
+            out_block(2 * d + 1 - at.r).start()
+        for d in order:
+            out_block(2 * d + at.r).start()
+        return 0
+
+    lax.fori_loop(1, at.depth + 1, fetch, 0)
     load_fc.start()
     load_lm.start()
     gain_buf[at.mine] = jnp.broadcast_to(own_gain[...], gain_buf.shape[1:])
     at.greet()
 
-    def span(q):
-        return pl.ds(pl.multiple_of(q * cols, cols), cols)
-
     def level(q):
         return gain_buf[q][:1]
 
     def multiply(q):
-        block = cap_buf[q]
-        captured[q] = block
-        total[...] += product(block, w_fc[span(q), :])
+        total[...] += product(cap_buf[q], w_fc[span(q), :])
 
     def head(q):
         state = feat_buf[q].astype(jnp.float32)
@@ -356,9 +375,13 @@
     caps = Gather(at, cap_buf, sems[6:12], multiply)
     feats = Gather(at, feat_buf, sems[12:18], head)
 
+    def first_part(q):
+        out_block(q).wait()
+        return product(context[...], w_out[:, span(q)])
+
     gains.start()
-    scatter_sum(
-        at, lambda q: product(context[...], w_out[:, span(q)]), narrow_plain, widen_plain,
+    drain_first = scatter_sum(
+        at, first_part, narrow_plain, widen_plain,
         buffers, sems[18:24], total,
     )
     cap_buf[at.mine] = (total[...] + residual[...].astype(jnp.float32)).astype(jnp.bfloat16)
@@ -366,19 +389,31 @@
     total[...] = fc_rest[...].astype(jnp.float32)
     moments[...] = jnp.zeros_like(moments)
     logits[...] = jnp.zeros_like(logits)
+    notes[...] = jnp.zeros_like(notes)
+    notes[0:1, : labels.shape[1]] = labels[...].astype(jnp.float32)
+    notes[1:2, : labels.shape[1]] = segments[...].astype(jnp.float32)
     gains.relay()
     load_fc.wait()
     caps.relay()
     caps.finish()
+    save = pltpu.make_async_copy(cap_buf, captured, load.at[2])
+    save.start()
     feat_buf[at.mine] = total[...].astype(jnp.bfloat16)
     feats.start()
     gains.finish()
     load_lm.wait()
+    columns_of = notes[...].T
+    now = columns_of[:, 1:2]
+    marks = [pltpu.roll(columns_of, columns_of.shape[0] - k, 0)[:rows] for k in (1, 2)]
+    usable_one, usable_two = [
+        jnp.where((mark[:, 0:1] >= 0.0) & (mark[:, 1:2] == now[:rows]), 1.0, 0.0) for mark in marks
+    ]
+    index = lax.broadcasted_iota(jnp.int32, (rows, 1), 0)
+    same = (pltpu.roll(columns_of, 1, 0)[:rows, 1:2] == now[:rows]) & (index > 0)
+    follows = jnp.broadcast_to(jnp.where(same, 1.0, 0.0), (rows, LANES))
     feats.relay()
     feats.finish()
 
-    follows = jnp.broadcast_to(flags[:, 0:1], (rows, LANES))
-    usable_one, usable_two = flags[:, 1:2], flags[:, 2:3]
     squares, mixed, squares_before = [spread_sum(moments[i]) / width for i in range(3)]
     scale_one = lax.rsqrt(squares + EPS)
     link = follows * earlier(scale_one)
@@ -393,7 +428,7 @@
     columns = lax.broadcasted_iota(jnp.int32, (rows, vocab_own), 1) + at.mine * vocab_own
 
     def matches(i):
-        return columns == marks[:, i : i + 1]
+        return columns == marks[i][:, 0:1].astype(jnp.int32)
 
     parts = [
         powers_one,
@@ -414,6 +449,8 @@
     stats[...] = packed.T[: stats.shape[0]]
     shared[at.mine] = stats[...]
 
+    drain_first()
+
     def share(k):
         q, target = at.other(k)
         return remote(stats, shared.at[at.mine], sems[30].at[q], sems[31].at[at.mine], target)
@@ -471,7 +508,7 @@
         gain_row = wide[rows : rows + 1] + wide[rows + 1 : rows + 2]
         return jnp.concatenate([wide[:rows], jnp.where(line == 0, gain_row, 0.0)], axis=0)
 
-    scatter_sum(at, part, narrow, widen, buffers, sems[24:30], summed)
+    drain_second = scatter_sum(at, part, narrow, widen, buffers, sems[24:30], summed)
 
     def average(totals, picked, usable):
         count = jnp.sum(usable, axis=0, keepdims=True)
@@ -505,14 +542,19 @@
         summed[:rows] - gain * pulled - state * pull_one[:, :1] - second * pull_two[:, :1]
     ).astype(jnp.bfloat16)
     grad_gain[...] = summed[rows : rows + 1] - jnp.sum(pulled * state, axis=0, keepdims=True)
-
-
-def whole_step(tensors, context, w_out, residual, fc_rest, w_fc, norm_gain, w_lm, marks, flags):
+    drain_second()
+    gains.drain()
+    caps.drain()
+    feats.drain()
+    save.wait()
+
+
+def whole_step(tensors, context, w_out, residual, fc_rest, w_fc, norm_gain, w_lm, labels, segments):
     rows = context.shape[0]
     width, cols = w_fc.shape
     vocab_own = w_lm.shape[1]
     blocks = 2 * tensors
-    tall = -(-rows // LANES) * LANES
+    tall = -(-(rows + 2) // LANES) * LANES
     far = pl.BlockSpec(memory_space=pl.ANY)
     return pl.pallas_call(
         functools.partial(step_kernel, tensors),
@@ -522,9 +564,10 @@
             jax.ShapeDtypeStruct((1, cols), jnp.float32),
             jax.ShapeDtypeStruct((1, LANES), jnp.float32),
         ),
-        in_specs=[in_vmem()] * 7 + [far] * 2,
-        out_specs=(in_vmem(),) * 4,
+        in_specs=[in_vmem()] * 6 + [far] * 3,
+        out_specs=(far,) + (in_vmem(),) * 3,
         scratch_shapes=[
+            pltpu.VMEM(w_out.shape, jnp.bfloat16),
             pltpu.VMEM((width, cols), jnp.bfloat16),
             pltpu.VMEM((vocab_own, width), jnp.bfloat16),
             pltpu.VMEM((rows, cols), jnp.float32),
@@ -537,7 +580,9 @@
             pltpu.VMEM((8, tall), jnp.float32),
             pltpu.VMEM((blocks, 8, tall), jnp.float32),
             pltpu.VMEM((rows + EXTRA, cols), jnp.float32),
-            pltpu.SemaphoreType.DMA((2,)),
+            pltpu.VMEM((LANES, tall), jnp.float32),
+            pltpu.SemaphoreType.DMA((3,)),
+            pltpu.SemaphoreType.DMA((blocks,)),
         ]
         + scatter_scratch(tensors, rows + EXTRA, cols)
         + gather_sems(tensors) * 3
@@ -546,31 +591,20 @@
         compiler_params=pltpu.CompilerParams(
             collective_id=0, has_side_effects=True, vmem_limit_bytes=VMEM_BYTES
         ),
-    )(context, w_out, residual, fc_rest, norm_gain[None, :], marks, flags, w_fc, w_lm.T)
+    )(
+        context, residual, fc_rest, norm_gain[None, :], labels[None, :], segments[None, :],
+        w_out, w_fc, w_lm.T,
+    )
 
 
 def on_device(
     context, w_out, residual, fc_rest, w_fc, norm_gain, w_lm, tokens, segments, vocab_map
 ):
     tensors = lax.axis_size("tensor")
-    rows = tokens.shape[0] - 2
     width, cols = w_fc.shape
-    seg_now = segments[:rows]
-    follows = jnp.concatenate(
-        [
-            jnp.zeros((1,), jnp.float32),
-            (segments[1:rows] == segments[: rows - 1]).astype(jnp.float32),
-        ]
-    )
-    labels_all = vocab_map[tokens]
-    labels = [labels_all[shift : shift + rows] for shift in (1, 2)]
-    usable = [
-        ((labels[k - 1] >= 0) & (segments[k : k + rows] == seg_now)).astype(jnp.float32)
-        for k in (1, 2)
-    ]
     captured, grad_state, grad_gain, losses = whole_step(
         tensors, context, w_out, residual, fc_rest, w_fc, norm_gain, w_lm,
-        jnp.stack(labels, axis=1), jnp.stack([follows] + usable, axis=1),
+        vocab_map[tokens], segments,
     )
     grad_fc = (
         jnp.einsum("pti,tj->pij", captured, grad_state, preferred_element_type=jnp.float32)

time: 133 us -> 132 us (level)
  other arithmetic: 2.49 us -> 0.75 us
    another operation x5 -> x0, local copies, waits for them, and re-layouts: 1.52 us -> none  [the longest x4 0.76 us: on_device(): jnp.stack([follows] + usable, axis=1)]
where the time goes in v4:
time: 132 us; the launch traced here: 131 us
  Pallas kernels  118 us (89%)
  matrix products  7.52 us (6%)
  local copies, waits for them, and re-layouts  3.99 us (3%)
    pallas_call x1, Pallas kernels, whole_step(): pl.pallas_call(functools.partial(step_kernel, tensors), out_shape=(jax.Sh...  118 us
    dot_general x1, matrix products, on_device(): jnp.einsum('pti,tj->pij', captured, grad_state, preferred_element_type=jn...  7.52 us

profile of v4, /device:TPU:0, one launch (start us, length us, event | category | flops | bytes accessed | tf_op | source)
XLA Modules:
  0.0 131.3 jit_solution(18352680579507696239)
XLA Ops:
  0.6 0.0 copy-start
  0.6 0.7 compare_select_fusion
  1.4 0.3 copy-done
  1.7 2.0 %gather_fusion = s32[162]{0:T(256)} fusion(s32[128256]{0:T(1024)S(1)} %copy-done, s32[1024]{0:T(1024)S(1)} %pad_clamp_fusion), kind=kCustom, calls=%fused_computation | custom fusion | bytes 1944 | tf_op jit(solution)/shard_map/gather | solution.py:607
  3.7 118.4 %shard_map.121 = (bf16[16,160,512]{2,1,0:T(8,128)(2,1)}, bf16[160,512]{1,0:T(8,128)(2,1)}, f32[1,512]{1,0:T(1,128)}, f32[1,128]{1,0:T(1,128)}) custom-call(bf16[160,512]{1,0:T(8,128)(2,1)} %context.1, bf16[160,512]{1,0:T(8,128)(2,1)} %residual.1, bf16[160,512]{1,0:T(8,128)(2,1)} %fc_rest.1, f32[1,512]{1,0:T(1,128)} %bitcast.15, s32[1,162]{1,0:T(1,128)} %bitcast.14, ...), custom_call_target="tpu_custom_call" | custom-call | tf_op jit(solution)/shard_map/pallas_call | solution.py:559
  122.1 0.0 copy-start.1
  122.1 1.1 slice_bitcast_fusion
  123.2 7.5 %convolution_convert_fusion = bf16[16,512,512]{2,1,0:T(8,128)(2,1)} fusion(bf16[16,160,512]{2,1,0:T(8,128)(2,1)} %get-tuple-element.8, bf16[160,512]{1,0:T(8,128)(2,1)} %get-tuple-element.9), kind=kOutput, calls=%fused_computation.1 | convolution fusion | flops 1346371584 | bytes 11173888 | tf_op jit(solution)/shard_map/pti,tj->pij/dot_general | solution.py:610
  130.7 0.0 copy-done.1
  130.7 0.6 copy.14
  (1 shorter events, 0.0 us)
Async XLA Ops:
  0.6 1.1 copy-start
  122.1 8.6 %copy-start.1 = (f32[1,512]{1,0:T(1,128)S(1)}, f32[1,512]{1,0:T(1,128)}, u32[]{:S(2)}) copy-start(f32[1,512]{1,0:T(1,128)} %get-tuple-element.10) | copy-start | bytes 6148

commit v5 on v4

--- a/solution.py
+++ b/solution.py
@@ -348,10 +348,9 @@
         return 0
 
     lax.fori_loop(1, at.depth + 1, fetch, 0)
-    load_fc.start()
-    load_lm.start()
     gain_buf[at.mine] = jnp.broadcast_to(own_gain[...], gain_buf.shape[1:])
     at.greet()
+    load_fc.start()
 
     def level(q):
         return gain_buf[q][:1]
@@ -386,6 +385,7 @@
     )
     cap_buf[at.mine] = (total[...] + residual[...].astype(jnp.float32)).astype(jnp.bfloat16)
     caps.start()
+    load_lm.start()
     total[...] = fc_rest[...].astype(jnp.float32)
     moments[...] = jnp.zeros_like(moments)
     logits[...] = jnp.zeros_like(logits)
@@ -562,7 +562,7 @@
             jax.ShapeDtypeStruct((blocks, rows, cols), jnp.bfloat16),
             jax.ShapeDtypeStruct((rows, cols), jnp.bfloat16),
             jax.ShapeDtypeStruct((1, cols), jnp.float32),
-            jax.ShapeDtypeStruct((1, LANES), jnp.float32),
+            jax.ShapeDtypeStruct((1, 2), jnp.float32),
         ),
         in_specs=[in_vmem()] * 6 + [far] * 3,
         out_specs=(far,) + (in_vmem(),) * 3,
@@ -611,7 +611,7 @@
         .astype(jnp.bfloat16)
         .reshape(width, cols)
     )
-    return (losses[0, :2], grad_fc, grad_gain[0])
+    return (losses[0], grad_fc, grad_gain[0])
 
 
 def solution(mesh):

time: 132 us -> 131 us (level)
  no operation moved by 1% of the time
where the time goes in v5:
time: 131 us
  Pallas kernels  118 us (90%)
  matrix products  7.52 us (6%)
  local copies, waits for them, and re-layouts  3.43 us (3%)
    pallas_call x1, Pallas kernels, whole_step(): pl.pallas_call(functools.partial(step_kernel, tensors), out_shape=(jax.Sh...  118 us
    dot_general x1, matrix products, on_device(): jnp.einsum('pti,tj->pij', captured, grad_state, preferred_element_type=jn...  7.52 us

profile of v5, /device:TPU:0, one launch (start us, length us, event | category | flops | bytes accessed | tf_op | source)
XLA Modules:
  0.0 130.8 jit_solution(457367788987689007)
XLA Ops:
  0.6 0.0 copy-start
  0.6 0.7 compare_select_fusion
  1.4 0.3 copy-done
  1.7 2.0 %gather_fusion = s32[162]{0:T(256)} fusion(s32[128256]{0:T(1024)S(1)} %copy-done, s32[1024]{0:T(1024)S(1)} %pad_clamp_fusion), kind=kCustom, calls=%fused_computation | custom fusion | bytes 1944 | tf_op jit(solution)/shard_map/gather | solution.py:607
  3.7 118.4 %shard_map.121 = (bf16[16,160,512]{2,1,0:T(8,128)(2,1)}, bf16[160,512]{1,0:T(8,128)(2,1)}, f32[1,512]{1,0:T(1,128)}, f32[1,2]{1,0:T(1,128)}) custom-call(bf16[160,512]{1,0:T(8,128)(2,1)} %context.1, bf16[160,512]{1,0:T(8,128)(2,1)} %residual.1, bf16[160,512]{1,0:T(8,128)(2,1)} %fc_rest.1, f32[1,512]{1,0:T(1,128)} %bitcast.14, s32[1,162]{1,0:T(1,128)} %bitcast.13, ...), custom_call_target="tpu_custom_call" | custom-call | tf_op jit(solution)/shard_map/pallas_call | solution.py:559
  122.1 0.0 copy-start.2
  122.2 0.0 copy-start.1
  122.2 7.5 %convolution_convert_fusion = bf16[16,512,512]{2,1,0:T(8,128)(2,1)} fusion(bf16[16,160,512]{2,1,0:T(8,128)(2,1)} %get-tuple-element.8, bf16[160,512]{1,0:T(8,128)(2,1)} %get-tuple-element.9), kind=kOutput, calls=%fused_computation.1 | convolution fusion | flops 1346371584 | bytes 11173888 | tf_op jit(solution)/shard_map/pti,tj->pij/dot_general | solution.py:610
  129.7 0.0 copy-done.2
  129.7 0.5 copy.15
  130.2 0.0 copy-done.1
  130.2 0.6 copy.16
  (1 shorter events, 0.0 us)
Async XLA Ops:
  0.6 1.1 copy-start
  122.1 7.5 %copy-start.2 = (f32[1,2]{1,0:T(1,128)S(1)}, f32[1,2]{1,0:T(1,128)}, u32[]{:S(2)}) copy-start(f32[1,2]{1,0:T(1,128)} %get-tuple-element.7) | copy-start | bytes 28
  122.2 8.1 %copy-start.1 = (f32[1,512]{1,0:T(1,128)S(1)}, f32[1,512]{1,0:T(1,128)}, u32[]{:S(2)}) copy-start(f32[1,512]{1,0:T(1,128)} %get-tuple-element.10) | copy-start | bytes 6148
